TPU v7x, 512 devices: a whole 4x4x16 slice. The times are simulated.
512 devices in a mesh: ep: 64 (over y, z), tp: 8 (over x, core).
Axes of the slice: x: 4, y: 4, z: 16, core: 2. Of those that a mesh axis runs over, the one named last changes fastest.
Arguments:
- tokens: bfloat16 [8192, 4096], P('ep', 'tp'), may hold values from -6 to 6
- routes: int32 [8192, 8], P('ep'), may hold values from 0 to 127, as said below
- gates: float32 [8192, 8], P('ep'), may hold values from 0.02 to 0.5
- up_weight: bfloat16 [128, 4096, 1024], P('ep', 'tp'), may hold values from -0.09375 to 0.09375
- replica_on: int32 [128], replicated, may hold values from 0 to 1, as said below
- grad_out: bfloat16 [8192, 1024], P('ep', 'tp'), may hold values from -6 to 6
Outputs:
- mixed: bfloat16 [8192, 1024], P('ep', 'tp')
- grad_tokens: bfloat16 [8192, 4096], P('ep', 'tp')
- grad_gates: float32 [8192, 8], P('ep')
- grad_up: bfloat16 [128, 4096, 1024], P('ep', 'tp')
Inputs may be any that keep to these rules, and one draw needn't show every extreme that they name: `routes`: each row names 8 different experts; every expert is named by some row. `replica_on`: of the experts j * 2 to (j + 1) * 2 - 1, exactly one has value 1, for every j.
All inputs are finite; a program needn't handle non-finite values.
Results may differ from a plain program's by a relative error of at most 0.0095.
Values may be sent and summed in bfloat16 or wider, within the bound.
A program may use at most 64 MiB of HBM per device.

v0:
```python
import jax
import jax.numpy as jnp
from jax import lax
from jax.sharding import PartitionSpec as P


def from_behind(value, axis, steps):
    count = lax.axis_size(axis)
    pairs = [(source, (source + steps) % count) for source in range(count)]
    return lax.ppermute(value, axis, pairs)


def derivative(hidden):
    sig = jax.nn.sigmoid(hidden)
    return sig * (1.0 + hidden * (1.0 - sig))


def on_device(tokens, routes, gates, up_weight, replica_on, grad_out):
    count, feat = tokens.shape
    topk = routes.shape[1]
    experts = replica_on.shape[0]
    local = up_weight.shape[0]
    share = grad_out.shape[1]
    n_ep = lax.axis_size("ep")
    half_dev = n_ep // 2
    half_exp = experts // 2
    capacity = 3 * count * topk // (4 * experts)
    pairs = count * topk
    width = 2 * capacity
    total = experts * width
    flat = routes.reshape(pairs)
    onehot = (flat[:, None] == jnp.arange(experts, dtype=jnp.int32)[None, :]).astype(jnp.int32)
    before = jnp.cumsum(onehot, 0) - onehot
    rank = jnp.sum(before * onehot, 1)
    copies = 1 + jnp.sum(onehot * replica_on[None, :], 1)
    copy_index = rank % copies
    slot = rank // copies
    kept = slot < capacity
    target = jnp.where(copy_index == 0, flat, (flat + half_exp) % experts)
    position = jnp.where(kept, target * width + copy_index * capacity + slot, total)
    match = position[None, :] == jnp.arange(total, dtype=jnp.int32)[:, None]
    table = jnp.sum(jnp.where(match, jnp.arange(pairs, dtype=jnp.int32)[None, :], 0), 1)
    table = table + jnp.where(jnp.any(match, 1), 0, pairs).astype(jnp.int32)
    padded_x = jnp.concatenate([tokens, jnp.zeros((1, feat), tokens.dtype)], 0)
    sent_rows = padded_x[table // topk].reshape(experts, width, feat)
    received = lax.all_to_all(sent_rows, "ep", split_axis=0, concat_axis=0, tiled=True).reshape(
        n_ep, local, 2, capacity, feat
    )
    up_copy = from_behind(up_weight, "ep", half_dev)
    up_both = jnp.stack([up_weight, up_copy])
    partial_value = jnp.einsum(
        "nescd,sedf->nescf", received, up_both, preferred_element_type=jnp.float32
    )
    hidden_full = lax.psum(partial_value, "tp")
    start = lax.axis_index("tp") * share
    hidden = lax.dynamic_slice_in_dim(hidden_full, start, share, 4)
    act_share = jax.nn.silu(hidden).astype(jnp.bfloat16).reshape(n_ep * local, width, share)
    returned = lax.all_to_all(act_share, "ep", split_axis=0, concat_axis=0, tiled=True).reshape(
        total, share
    )
    returned = jnp.concatenate([returned, jnp.zeros((1, share), jnp.bfloat16)], 0)
    act_pairs = returned[position].reshape(count, topk, share).astype(jnp.float32)
    mixed = jnp.einsum("tk,tkf->tf", gates, act_pairs).astype(jnp.bfloat16)
    gate_part = jnp.einsum("tkf,tf->tk", act_pairs, grad_out.astype(jnp.float32))
    grad_gates = lax.psum(gate_part, "tp")
    row_grad = (gates[:, :, None] * grad_out[:, None, :].astype(jnp.float32)).astype(jnp.bfloat16)
    padded_g = jnp.concatenate(
        [row_grad.reshape(pairs, share), jnp.zeros((1, share), jnp.bfloat16)], 0
    )
    sent_grads = padded_g[table].reshape(experts, width, share)
    grads_in = lax.all_to_all(sent_grads, "ep", split_axis=0, concat_axis=0, tiled=True).reshape(
        n_ep, local, 2, capacity, share
    )
    grad_part = (grads_in.astype(jnp.float32) * derivative(hidden)).astype(jnp.bfloat16)
    hidden_grad = lax.all_gather(grad_part, "tp", axis=4, tiled=True)
    up_grads = jnp.einsum(
        "nescd,nescf->sedf", received, hidden_grad, preferred_element_type=jnp.float32
    )
    input_rows = jnp.einsum(
        "nescf,sedf->nescd", hidden_grad, up_both, preferred_element_type=jnp.float32
    ).astype(jnp.bfloat16)
    input_rows = input_rows.reshape(n_ep * local, width, feat)
    back_rows = lax.all_to_all(input_rows, "ep", split_axis=0, concat_axis=0, tiled=True).reshape(
        total, feat
    )
    back_rows = jnp.concatenate([back_rows, jnp.zeros((1, feat), jnp.bfloat16)], 0)
    input_pairs = back_rows[position].reshape(count, topk, feat)
    grad_tokens = jnp.sum(input_pairs.astype(jnp.float32), 1).astype(jnp.bfloat16)
    up_back = from_behind(up_grads[1], "ep", half_dev)
    grad_up = (up_grads[0] + up_back).astype(jnp.bfloat16)
    return (mixed, grad_tokens, grad_gates, grad_up)


def solution(mesh):
    return jax.shard_map(
        on_device,
        mesh=mesh,
        in_specs=(
            P("ep", "tp"),
            P("ep", None),
            P("ep", None),
            P("ep", "tp", None),
            P(),
            P("ep", "tp"),
        ),
        out_specs=(P("ep", "tp"), P("ep", "tp"), P("ep", None), P("ep", "tp", None)),
        check_vma=False,
    )
```

profile of v0, /device:TPU:1, one launch (start us, length us, event | category | flops | bytes accessed | tf_op | source)
XLA Modules:
  0.0 450.8 jit_solution(9975775816436484200)
XLA Ops:
  7.2 0.8 copy.76
  8.0 0.1 eq.73
  8.1 0.1 eq.77
  8.2 0.1 copy.78
  8.3 0.2 fusion.15
  8.6 0.1 copy.79
  8.7 1.2 select_reduce_fusion.1
  9.8 0.1 broadcast_add_fusion.1
  10.0 0.8 fusion
  10.8 0.7 select_reduce_fusion
  11.5 0.1 fusion.23
  11.6 4.8 %gather_fusion = bf16[1536,512]{1,0:T(8,128)(2,1)S(1)} fusion(bf16[129,512]{1,0:T(8,128)(2,1)S(1)} %concatenate.12, s32[2048]{0:T(1024)S(1)} %get-tuple-element.13), kind=kCustom, calls=%fused_computation | custom fusion | bytes 3151872 | tf_op jit(solution)/shard_map/gather | solution.py:45
  16.5 1.5 reshape.356
  18.0 19.3 %all-to-all-start = ((bf16[128,12,512]{2,1,0:T(8,128)(2,1)}), bf16[128,12,512]{2,1,0:T(8,128)(2,1)S(1)}, u32[]{:S(2)}, u32[]{:S(2)}) async-start(bf16[128,12,512]{2,1,0:T(8,128)(2,1)} %reshape.356), calls=%async_computation | async-start | bytes 4194304 | tf_op jit(solution)/shard_map/all_to_all | solution.py:46
  37.3 0.0 all-reduce.6.cloned.1.call-start
  37.3 4.5 %collective-permute-start = (bf16[2,512,1024]{2,1,0:T(8,128)(2,1)}, bf16[2,512,1024]{2,1,0:T(8,128)(2,1)}, u32[]{:S(2)}, u32[]{:S(2)}) collective-permute-start(bf16[2,512,1024]{2,1,0:T(8,128)(2,1)} %param.9), channel_id=1, source_target_pairs={{0,256},{8,264},{16,272},{24,280},{32,288},{40,296},{48,304},{56,3... | collective-permute-start | bytes 6291464 | tf_op jit(solution)/shard_map/ppermute | solution.py:10
  41.8 90.2 %all-to-all-done = bf16[128,12,512]{2,1,0:T(8,128)(2,1)S(1)} async-done(((bf16[128,12,512]{2,1,0:T(8,128)(2,1)}), bf16[128,12,512]{2,1,0:T(8,128)(2,1)S(1)}, u32[]{:S(2)}, u32[]{:S(2)}) %all-to-all-start) | async-done | bytes 1572896 | tf_op jit(solution)/shard_map/all_to_all | solution.py:46
  132.1 2.0 copy.80
  134.1 2.5 reshape.357
  136.6 0.0 copy-start.1
  136.6 0.0 collective-permute-done
  136.6 7.2 %fusion.6 = f32[64,2,2,6,1024]{4,0,3,2,1:T(8,128)} fusion(bf16[1,2,512,1024]{3,2,0,1:T(8,128)(2,1)} %bitcast.1, bf16[1,2,512,1024]{3,2,0,1:T(8,128)(2,1)} %bitcast.75, bf16[64,2,2,6,512]{4,1,0,3,2:T(2,128)(2,1)S(1)} %reshape.357), kind=kOutput, calls=%fused_computation.16 | convolution fusion | flops 1619001344 | bytes 12058624 | tf_op jit(solution)/shard_map/nescd,sedf->nescf/dot_general | solution.py:51
  143.8 0.0 all-reduce.6.cloned.1.call-update
  143.9 0.7 copy-done.4
  144.5 0.1 copy.85
  144.6 0.1 mul.93
  144.7 0.2 fusion.14
  145.0 3.2 gather_fusion.2
  148.2 0.9 reshape.362
  149.1 10.9 %all-to-all-start.2 = ((bf16[128,12,128]{2,1,0:T(8,128)(2,1)}), bf16[128,12,128]{2,1,0:T(8,128)(2,1)S(1)}, u32[]{:S(2)}, u32[]{:S(2)}) async-start(bf16[128,12,128]{2,1,0:T(8,128)(2,1)} %reshape.362), calls=%async_computation.2 | async-start | bytes 1048576 | tf_op jit(solution)/shard_map/all_to_all | solution.py:71
  160.0 0.0 all-gather.2.cloned.1.call-start
  160.0 29.4 %all-to-all-done.2 = bf16[128,12,128]{2,1,0:T(8,128)(2,1)S(1)} async-done(((bf16[128,12,128]{2,1,0:T(8,128)(2,1)}), bf16[128,12,128]{2,1,0:T(8,128)(2,1)S(1)}, u32[]{:S(2)}, u32[]{:S(2)}) %all-to-all-start.2) | async-done | bytes 393248 | tf_op jit(solution)/shard_map/all_to_all | solution.py:71
  189.5 0.1 copy.100
  189.5 50.6 %all-reduce.6.cloned.1.call-done = f32[64,2,2,6,1024]{4,0,3,2,1:T(8,128)} async-done(((f32[64,2,2,6,1024]{4,0,3,2,1:T(8,128)}), f32[64,2,2,6,1024]{4,0,3,2,1:T(8,128)}) %all-reduce.6.cloned.1.call-update) | async-done | bytes 6291472 | tf_op jit(solution)/shard_map/psum | solution.py:54
  240.2 2.3 fusion.11
  242.5 0.0 all-gather.2.cloned.1.call-update
  242.5 0.4 copy.82
  242.9 1.1 copy.83
  244.0 15.4 %all-to-all-start.1 = ((bf16[128,12,128]{2,1,0:T(8,128)(2,1)}), bf16[128,12,128]{2,1,0:T(8,128)(2,1)S(1)}, u32[]{:S(2)}, u32[]{:S(2)}) async-start(bf16[128,12,128]{2,1,0:T(8,128)(2,1)} %copy.83), calls=%async_computation.1 | async-start | bytes 1048576 | tf_op jit(solution)/shard_map/all_to_all | solution.py:58
  259.4 23.2 %all-gather.2.cloned.1.call-done = bf16[64,2,2,6,1024]{4,0,3,2,1:T(8,128)(2,1)} async-done(((bf16[64,2,2,6,128]{4,0,3,2,1:T(8,128)(2,1)}), bf16[64,2,2,6,1024]{4,0,3,2,1:T(8,128)(2,1)}) %all-gather.2.cloned.1.call-update) | async-done | bytes 3145744 | tf_op jit(solution)/shard_map/all_gather | solution.py:75
  282.6 5.0 %fusion.10 = bf16[64,2,2,6,512]{4,0,3,2,1:T(8,128)(2,1)S(1)} fusion(bf16[64,2,2,6,1024]{4,0,3,2,1:T(8,128)(2,1)} %all-gather.2.cloned.1.call-done, bf16[1,2,512,1024]{3,2,0,1:T(8,128)(2,1)} %bitcast.1, bf16[1,2,512,1024]{3,2,0,1:T(8,128)(2,1)} %bitcast.76), kind=kOutput, calls=%fused_computation.20 | convolution fusion | flops 1619787776 | bytes 8912896 | tf_op jit(solution)/shard_map/nescf,sedf->nescd/dot_general | solution.py:79
  287.7 0.9 copy.98
  288.6 2.1 reshape.405
  290.7 0.0 all-to-all-done.1
  290.7 15.4 %all-to-all-start.3 = ((bf16[128,12,512]{2,1,0:T(8,128)(2,1)}), bf16[128,12,512]{2,1,0:T(8,128)(2,1)S(1)}, u32[]{:S(2)}, u32[]{:S(2)}) async-start(bf16[128,12,512]{2,1,0:T(8,128)(2,1)} %reshape.405), calls=%async_computation.3 | async-start | bytes 4194304 | tf_op jit(solution)/shard_map/all_to_all | solution.py:83
  306.1 4.7 %convolution_bitcast_fusion = f32[2,2,512,1024]{3,2,1,0:T(8,128)S(1)} fusion(bf16[64,2,2,6,1024]{4,0,3,2,1:T(8,128)(2,1)} %all-gather.2.cloned.1.call-done, bf16[64,2,2,6,512]{4,1,0,3,2:T(2,128)(2,1)} %copy-done.1), kind=kOutput, calls=%fused_computation.12 | convolution fusion | flops 1610612736 | bytes 13107200 | tf_op jit(solution)/shard_map/nescd,nescf->sedf/dot_general | solution.py:76
  310.8 2.9 slice_bitcast_fusion
  313.7 1.6 copy-done
  315.3 4.5 %collective-permute-start.1 = (f32[2,512,1024]{2,1,0:T(8,128)}, f32[2,512,1024]{2,1,0:T(8,128)}, u32[]{:S(2)}, u32[]{:S(2)}) collective-permute-start(f32[2,512,1024]{2,1,0:T(8,128)} %slice_bitcast_fusion), channel_id=1, source_target_pairs={{0,256},{8,264},{16,272},{24,280},{32,288},{40,296},{48,304},{56,3... | collective-permute-start | bytes 12582920 | tf_op jit(solution)/shard_map/ppermute | solution.py:10
  319.8 0.1 reshape.360
  319.9 0.1 copy.93
  320.0 0.7 compare_select_fusion.1
  320.8 0.1 reshape.359
  320.9 3.2 gather_fusion.1
  324.1 0.3 fusion.17
  324.4 0.3 fusion.19
  324.8 0.6 convert_element_type.46
  325.4 13.8 %psum.15 = f32[128,8]{0,1:T(8,128)} all-reduce(f32[128,8]{0,1:T(8,128)S(1)} %bitcast.72), channel_id=1, replica_groups=mesh['ep'=64,'tp'=8] {'tp'}, use_global_device_ids=true, to_apply=%region_8.9 | all-reduce | flops 1024 | bytes 8192 | tf_op jit(solution)/shard_map/psum | solution.py:65
  339.2 91.1 %collective-permute-done.1 = f32[2,512,1024]{2,1,0:T(8,128)} collective-permute-done((f32[2,512,1024]{2,1,0:T(8,128)}, f32[2,512,1024]{2,1,0:T(8,128)}, u32[]{:S(2)}, u32[]{:S(2)}) %collective-permute-start.1) | collective-permute-done | bytes 4194336 | tf_op jit(solution)/shard_map/ppermute | solution.py:10
  430.3 5.5 %fusion.2 = bf16[2,512,1024]{2,1,0:T(8,128)(2,1)} fusion(f32[2,512,1024]{2,1,0:T(8,128)} %collective-permute-done.1, f32[2,2,512,1024]{3,2,1,0:T(8,128)} %copy-done), kind=kLoop, calls=%fused_computation.10 | loop fusion | flops 2097152 | bytes 10485760 | tf_op jit(solution)/shard_map/convert_element_type | solution.py:90
  435.8 1.3 reshape.364
  437.2 1.5 concatenate.15
  438.7 4.0 gather_fusion.3
  442.6 1.3 bitcast_reduce_fusion
  (20 shorter events, 0.2 us)
Async XLA Ops:
  7.2 4.4 copy-start.2
  18.0 114.1 %all-to-all-start = ((bf16[128,12,512]{2,1,0:T(8,128)(2,1)}), bf16[128,12,512]{2,1,0:T(8,128)(2,1)S(1)}, u32[]{:S(2)}, u32[]{:S(2)}) async-start(bf16[128,12,512]{2,1,0:T(8,128)(2,1)} %reshape.356), calls=%async_computation | async-start | bytes 4194304 | tf_op jit(solution)/shard_map/all_to_all | solution.py:46
  37.3 202.9 %all-reduce.6.cloned.1.call-start = ((), (), s32[]{:S(2)}) async-start(), calls=%async_computation.4 | async-start | bytes 12582912 | tf_op jit(solution)/shard_map/psum | solution.py:54
  37.3 99.3 %collective-permute-start = (bf16[2,512,1024]{2,1,0:T(8,128)(2,1)}, bf16[2,512,1024]{2,1,0:T(8,128)(2,1)}, u32[]{:S(2)}, u32[]{:S(2)}) collective-permute-start(bf16[2,512,1024]{2,1,0:T(8,128)(2,1)} %param.9), channel_id=1, source_target_pairs={{0,256},{8,264},{16,272},{24,280},{32,288},{40,296},{48,304},{56,3... | collective-permute-start | bytes 6291464 | tf_op jit(solution)/shard_map/ppermute | solution.py:10
  136.6 7.3 %copy-start.1 = (bf16[64,2,2,6,512]{4,1,0,3,2:T(2,128)(2,1)}, bf16[64,2,2,6,512]{4,1,0,3,2:T(2,128)(2,1)S(1)}, u32[]{:S(2)}) copy-start(bf16[64,2,2,6,512]{4,1,0,3,2:T(2,128)(2,1)S(1)} %reshape.357) | copy-start | bytes 4718596
  143.8 0.7 copy-start.4
  143.8 0.9 copy-start.3
  149.1 40.4 %all-to-all-start.2 = ((bf16[128,12,128]{2,1,0:T(8,128)(2,1)}), bf16[128,12,128]{2,1,0:T(8,128)(2,1)S(1)}, u32[]{:S(2)}, u32[]{:S(2)}) async-start(bf16[128,12,128]{2,1,0:T(8,128)(2,1)} %reshape.362), calls=%async_computation.2 | async-start | bytes 1048576 | tf_op jit(solution)/shard_map/all_to_all | solution.py:71
  160.0 122.7 %all-gather.2.cloned.1.call-start = ((), (), s32[]{:S(2)}) async-start(), calls=%async_computation.5 | async-start | bytes 3538944 | tf_op jit(solution)/shard_map/all_gather | solution.py:75
  244.0 46.7 %all-to-all-start.1 = ((bf16[128,12,128]{2,1,0:T(8,128)(2,1)}), bf16[128,12,128]{2,1,0:T(8,128)(2,1)S(1)}, u32[]{:S(2)}, u32[]{:S(2)}) async-start(bf16[128,12,128]{2,1,0:T(8,128)(2,1)} %copy.83), calls=%async_computation.1 | async-start | bytes 1048576 | tf_op jit(solution)/shard_map/all_to_all | solution.py:58
  290.7 145.1 %all-to-all-start.3 = ((bf16[128,12,512]{2,1,0:T(8,128)(2,1)}), bf16[128,12,512]{2,1,0:T(8,128)(2,1)S(1)}, u32[]{:S(2)}, u32[]{:S(2)}) async-start(bf16[128,12,512]{2,1,0:T(8,128)(2,1)} %reshape.405), calls=%async_computation.3 | async-start | bytes 4194304 | tf_op jit(solution)/shard_map/all_to_all | solution.py:83
  310.8 4.5 copy-start
  315.3 115.0 %collective-permute-start.1 = (f32[2,512,1024]{2,1,0:T(8,128)}, f32[2,512,1024]{2,1,0:T(8,128)}, u32[]{:S(2)}, u32[]{:S(2)}) collective-permute-start(f32[2,512,1024]{2,1,0:T(8,128)} %slice_bitcast_fusion), channel_id=1, source_target_pairs={{0,256},{8,264},{16,272},{24,280},{32,288},{40,296},{48,304},{56,3... | collective-permute-start | bytes 12582920 | tf_op jit(solution)/shard_map/ppermute | solution.py:10
Sparse Core Ops, SparseCore 0:
  144.0 96.1 all-reduce.5
  242.6 39.9 all-gather.1
where the time goes:
time: 452 us; the launch traced here: 451 us
  waiting for transfers between devices  285 us (63%)
  starting transfers between devices  70 us (15%)
  local copies, waits for them, and re-layouts  36.5 us (8%)
  matrix products  17.6 us (4%)
  between operations  14.4 us (3%)
  other arithmetic  13.9 us (3%)
  blocking collectives  13.8 us (3%)
    ppermute x2, waiting for transfers between devices, from_behind(): return lax.ppermute(value, axis, pairs)  91.1 us
    all_to_all x1, waiting for transfers between devices, on_device(): lax.all_to_all(sent_rows, 'ep', split_axis=0, concat_axis=0, tiled=True)  90.2 us
    psum x1, waiting for transfers between devices, on_device(): hidden_full = lax.psum(partial_value, 'tp')  50.6 us
    all_to_all x1, waiting for transfers between devices, on_device(): lax.all_to_all(sent_grads, 'ep', split_axis=0, concat_axis=0, tiled=True)  29.4 us
    all_gather x1, waiting for transfers between devices, on_device(): hidden_grad = lax.all_gather(grad_part, 'tp', axis=4, tiled=True)  23.2 us
    all_to_all x1, starting transfers between devices, on_device(): lax.all_to_all(sent_rows, 'ep', split_axis=0, concat_axis=0, tiled=True)  19.3 us
    all_to_all x1, starting transfers between devices, on_device(): lax.all_to_all(act_share, 'ep', split_axis=0, concat_axis=0, tiled=True)  15.4 us
    all_to_all x1, starting transfers between devices, on_device(): lax.all_to_all(input_rows, 'ep', split_axis=0, concat_axis=0, tiled=True)  15.4 us
  transfers between devices with their start and end apart: 8, of which 5 were waited for; matrix products, arithmetic and copies ran while one was open for 8% of the time, Pallas kernels for 0%

commit v1 on v0

v1 whole, which is shorter than its diff:
```python
import jax
import jax.numpy as jnp
from jax import lax
from jax.sharding import PartitionSpec as P

CAP = 6
ROWS = 3 * CAP


def derivative(hidden):
    sig = jax.nn.sigmoid(hidden)
    return sig * (1.0 + hidden * (1.0 - sig))


def exact_dot(a, b):
    return jnp.dot(a, b, preferred_element_type=jnp.float32)


def on_device(tokens, routes, gates, up_weight, replica_on, grad_out):
    count, feat = tokens.shape
    topk = routes.shape[1]
    experts = replica_on.shape[0]
    n_ep = lax.axis_size("ep")
    total = n_ep * ROWS
    share = grad_out.shape[1]
    choice = routes[:, :, None] == jnp.arange(experts, dtype=jnp.int32)[None, None, :]
    names = jnp.sum(choice.astype(jnp.float32), 1)
    lower = jnp.tril(jnp.ones((count, count), jnp.bfloat16), -1)
    rank = exact_dot(lower, names.astype(jnp.bfloat16)).astype(jnp.int32)
    kept = rank < CAP * (1 + replica_on)[None, :]
    expert_ids = jnp.arange(experts, dtype=jnp.int32)
    base = (expert_ids // 2) * ROWS + jnp.where(replica_on == 1, 0, 2 * CAP)
    place = jnp.where(kept, rank + base[None, :], -1)
    position = jnp.sum(jnp.where(choice, place[:, None, :], 0), 2)
    row_ids = jnp.arange(total, dtype=jnp.int32)
    match = position[None, :, :] == row_ids[:, None, None]
    pick = jnp.any(match, 2).astype(jnp.bfloat16)
    gate_row = jnp.sum(jnp.where(match, gates[None, :, :], 0.0), (1, 2))
    sent = exact_dot(pick, tokens).astype(jnp.bfloat16).reshape(n_ep, ROWS, feat)
    grad_rows = exact_dot(pick, grad_out)
    sent_grads = (gate_row[:, None] * grad_rows).astype(jnp.bfloat16).reshape(n_ep, ROWS, share)
    received = lax.all_to_all(sent, "ep", split_axis=0, concat_axis=0, tiled=True)
    x_hot = received[:, : 2 * CAP].reshape(n_ep * 2 * CAP, feat)
    x_cold = received[:, 2 * CAP :].reshape(n_ep * CAP, feat)
    grads_in = lax.all_to_all(sent_grads, "ep", split_axis=0, concat_axis=0, tiled=True)
    hot_is_1 = replica_on[2 * lax.axis_index("ep") + 1] == 1
    w_hot = jnp.where(hot_is_1, up_weight[1], up_weight[0])
    w_cold = jnp.where(hot_is_1, up_weight[0], up_weight[1])
    partial_value = jnp.concatenate([exact_dot(x_hot, w_hot), exact_dot(x_cold, w_cold)], 0)
    hidden = lax.psum_scatter(partial_value, "tp", scatter_dimension=1, tiled=True)
    n_hot = n_ep * 2 * CAP

    def by_group(rows):
        return jnp.concatenate(
            [rows[:n_hot].reshape(n_ep, 2 * CAP, -1), rows[n_hot:].reshape(n_ep, CAP, -1)], 1
        )

    act = jax.nn.silu(hidden).astype(jnp.bfloat16)
    grads_flat = jnp.concatenate(
        [grads_in[:, : 2 * CAP].reshape(n_hot, share), grads_in[:, 2 * CAP :].reshape(-1, share)], 0
    )
    grad_part = (grads_flat.astype(jnp.float32) * derivative(hidden)).astype(jnp.bfloat16)
    hidden_grad = lax.all_gather(grad_part, "tp", axis=1, tiled=True)
    returned = lax.all_to_all(by_group(act), "ep", split_axis=0, concat_axis=0, tiled=True)
    returned = returned.reshape(total, share).astype(jnp.float32)
    mixed = lax.dot_general(
        pick.astype(jnp.float32),
        gate_row[:, None] * returned,
        (((0,), (0,)), ((), ())),
        precision=lax.Precision.HIGHEST,
        preferred_element_type=jnp.float32,
    ).astype(jnp.bfloat16)
    gate_part = jnp.sum(returned * grad_rows, 1)
    gate_pairs = jnp.sum(jnp.where(match, gate_part[:, None, None], 0.0), 0)
    grad_gates = lax.psum(gate_pairs, "tp")
    contract_f = (((1,), (1,)), ((), ()))
    back_hot = lax.dot_general(hidden_grad[:n_hot], w_hot, contract_f, preferred_element_type=jnp.float32)
    back_cold = lax.dot_general(hidden_grad[n_hot:], w_cold, contract_f, preferred_element_type=jnp.float32)
    input_rows = by_group(jnp.concatenate([back_hot, back_cold], 0).astype(jnp.bfloat16))
    back = lax.all_to_all(input_rows, "ep", split_axis=0, concat_axis=0, tiled=True).reshape(total, feat)
    contract_r = (((0,), (0,)), ((), ()))
    grad_tokens = lax.dot_general(pick, back, contract_r, preferred_element_type=jnp.float32).astype(jnp.bfloat16)
    g_hot = lax.dot_general(x_hot, hidden_grad[:n_hot], contract_r, preferred_element_type=jnp.float32)
    g_cold = lax.dot_general(x_cold, hidden_grad[n_hot:], contract_r, preferred_element_type=jnp.float32)
    grad_up = jnp.stack(
        [jnp.where(hot_is_1, g_cold, g_hot), jnp.where(hot_is_1, g_hot, g_cold)]
    ).astype(jnp.bfloat16)
    return (mixed, grad_tokens, grad_gates, grad_up)


def solution(mesh):
    return jax.shard_map(
        on_device,
        mesh=mesh,
        in_specs=(
            P("ep", "tp"),
            P("ep", None),
            P("ep", None),
            P("ep", "tp", None),
            P(),
            P("ep", "tp"),
        ),
        out_specs=(P("ep", "tp"), P("ep", "tp"), P("ep", None), P("ep", "tp", None)),
        check_vma=False,
    )
```

time: 452 us -> 385 us (0.85)
  waiting for transfers between devices: 285 us -> 199 us
  blocking collectives: 13.8 us -> 80 us
  starting transfers between devices: 70 us -> 34.9 us
  local copies, waits for them, and re-layouts: 36.5 us -> 8.44 us
  other arithmetic: 13.9 us -> 25.1 us
    ppermute x2 -> x0, waiting for transfers between devices: 91.1 us -> none  [from_behind(): return lax.ppermute(value, axis, pairs)]
    all_to_all x0 -> x2, blocking collectives: none -> 66.8 us  [the longest x1 35.5 us: on_device(): lax.all_to_all(by_group(act), 'ep', split_axis=0, concat_axis=0, tiled=True)]
    all_to_all x3 -> x1, waiting for transfers between devices: 120 us -> 69 us  [on_device(): lax.all_to_all(sent, 'ep', split_axis=0, concat_axis=0, tiled=True)]
    psum x1 -> x0, waiting for transfers between devices: 50.6 us -> none  [on_device(): hidden_full = lax.psum(partial_value, 'tp')]
    all_to_all x1, waiting for transfers between devices: 0.01 us -> 50.6 us  [on_device(): lax.all_to_all(input_rows, 'ep', split_axis=0, concat_axis=0, tiled=True)]
    reduce_scatter x0 -> x1, waiting for transfers between devices: none -> 43.2 us  [on_device(): lax.psum_scatter(partial_value, 'tp', scatter_dimension=1, tiled=True)]
    all_to_all x3 -> x1, starting transfers between devices: 45.5 us -> 19.4 us  [on_device(): lax.all_to_all(sent, 'ep', split_axis=0, concat_axis=0, tiled=True)]
    gather x4 -> x0, local copies, waits for them, and re-layouts: 15.2 us -> none  [the longest x1 4.81 us: on_device(): sent_rows = padded_x[table // topk].reshape(experts, width, feat)]
  transfers between devices with their start and end apart: 8 -> 4, of which waited for: 5 -> 4; matrix products, arithmetic and copies ran while one was open for 8% -> 2% of each run, Pallas kernels for 0% -> 0%
where the time goes in v1:
time: 385 us; the launch traced here: 380 us
  waiting for transfers between devices  199 us (52%)
  blocking collectives  80 us (21%)
  starting transfers between devices  34.9 us (9%)
  other arithmetic  25.1 us (7%)
  matrix products  17.5 us (5%)
  between operations  15 us (4%)
  local copies, waits for them, and re-layouts  8.44 us (2%)
    all_to_all x1, waiting for transfers between devices, on_device(): lax.all_to_all(sent, 'ep', split_axis=0, concat_axis=0, tiled=True)  69 us
    all_to_all x1, waiting for transfers between devices, on_device(): lax.all_to_all(input_rows, 'ep', split_axis=0, concat_axis=0, tiled=True)  50.6 us
    reduce_scatter x1, waiting for transfers between devices, on_device(): lax.psum_scatter(partial_value, 'tp', scatter_dimension=1, tiled=True)  43.2 us
    all_gather x1, waiting for transfers between devices, on_device(): hidden_grad = lax.all_gather(grad_part, 'tp', axis=1, tiled=True)  36.4 us
    all_to_all x1, blocking collectives, on_device(): lax.all_to_all(by_group(act), 'ep', split_axis=0, concat_axis=0, tiled=True)  35.5 us
    all_to_all x1, blocking collectives, on_device(): lax.all_to_all(sent_grads, 'ep', split_axis=0, concat_axis=0, tiled=True)  31.2 us
    all_to_all x1, starting transfers between devices, on_device(): lax.all_to_all(sent, 'ep', split_axis=0, concat_axis=0, tiled=True)  19.4 us
    all_to_all x1, starting transfers between devices, on_device(): lax.all_to_all(input_rows, 'ep', split_axis=0, concat_axis=0, tiled=True)  15.4 us
  transfers between devices with their start and end apart: 4, of which 4 were waited for; matrix products, arithmetic and copies ran while one was open for 2% of the time, Pallas kernels for 0%

profile of v1, /device:TPU:1, one launch (start us, length us, event | category | flops | bytes accessed | tf_op | source)
XLA Modules:
  0.0 380.3 jit_solution(6317620733446485928)
XLA Ops:
  7.2 0.0 copy-start
  7.2 0.7 add_multiply_fusion
  7.9 0.8 copy.14
  8.7 0.2 convert_reduce_fusion
  8.9 0.2 add_select_fusion
  9.1 2.4 select_reduce_fusion.2
  11.6 4.2 %fusion = pred[1152,128]{1,0:T(8,128)(4,1)S(1)} fusion(s32[128,8]{0,1:T(8,128)S(1)} %copy.15), kind=kLoop, calls=%fused_computation.4 | loop fusion | flops 2211840 | bytes 151552 | tf_op jit(solution)/shard_map/reduce_or | solution.py:37
  15.8 0.0 copy-done
  15.8 0.5 convolution_convert_fusion
  16.2 1.3 reshape.61
  17.6 0.0 copy-start.6
  17.6 19.4 %all-to-all-start = ((bf16[64,18,512]{2,1,0:T(8,128)(2,1)}), bf16[64,18,512]{2,1,0:T(8,128)(2,1)S(1)}, u32[]{:S(2)}, u32[]{:S(2)}) async-start(bf16[64,18,512]{2,1,0:T(8,128)(2,1)} %reshape.61), calls=%async_computation | async-start | bytes 3145728 | tf_op jit(solution)/shard_map/all_to_all | solution.py:42
  37.0 0.0 reduce-scatter.2.cloned.1.call-start
  37.0 0.0 copy-done.6
  37.1 0.6 dynamic_slice.3
  38.3 69.0 %all-to-all-done = bf16[64,18,512]{2,1,0:T(8,128)(2,1)S(1)} async-done(((bf16[64,18,512]{2,1,0:T(8,128)(2,1)}), bf16[64,18,512]{2,1,0:T(8,128)(2,1)S(1)}, u32[]{:S(2)}, u32[]{:S(2)}) %all-to-all-start) | async-done | bytes 1179680 | tf_op jit(solution)/shard_map/all_to_all | solution.py:42
  107.3 1.1 slice.52
  108.4 1.3 reshape.62
  109.7 0.2 slice.53
  109.9 0.9 reshape.63
  110.8 0.0 copy-start.2
  110.8 2.4 fusion.7
  113.2 0.0 copy-done.2
  113.2 1.0 fusion.10
  114.2 2.5 pad_maximum_fusion
  116.7 0.0 reduce-scatter.2.cloned.1.call-update
  116.7 0.0 all-gather.2.cloned.1.call-start
  116.8 43.2 %reduce-scatter.2.cloned.1.call-done = f32[1152,128]{1,0:T(8,128)} async-done(((f32[1152,1024]{1,0:T(8,128)}), f32[1152,128]{1,0:T(8,128)}) %reduce-scatter.2.cloned.1.call-update) | async-done | bytes 589840 | tf_op jit(solution)/shard_map/reduce_scatter | solution.py:50
  160.0 1.2 multiply_convert_fusion.2
  161.2 0.0 copy-start.4
  161.3 0.0 copy-start.5
  161.4 0.1 pad_maximum_fusion.3
  161.5 35.5 %all_to_all.20 = bf16[64,18,128]{2,1,0:T(8,128)(2,1)S(1)} all-to-all(bf16[64,18,128]{2,1,0:T(8,128)(2,1)S(1)} %pad_maximum_fusion.3), channel_id=1, replica_groups=mesh['ep'=64,'tp'=8] {'ep'}, dimensions={0} | all-to-all | bytes 589824 | tf_op jit(solution)/shard_map/all_to_all | solution.py:64
  197.1 0.1 reshape.72
  197.2 0.0 copy-done.4
  197.2 0.4 multiply_reduce_fusion
  197.6 0.0 copy-start.1
  197.6 0.0 copy-done.5
  197.6 9.5 %select_reduce_fusion = (f32[128,8]{0,1:T(8,128)S(1)}, f32[1152]{0:T(1024)S(1)}) fusion(f32[1152]{0:T(1024)S(1)} %get-tuple-element.10, s32[128,8]{0,1:T(8,128)S(1)} %copy.15, f32[128,8]{0,1:T(8,128)S(1)} %copy-done.5), kind=kLoop, calls=%fused_computation.1 | loop fusion | flops 5896064 | bytes 21504 | tf_op jit(solution)/shard_map/reduce_sum | solution.py:74
  207.1 0.2 multiply_convert_fusion.1
  207.3 0.1 reshape.66
  207.4 31.2 %all_to_all.21 = bf16[64,18,128]{2,1,0:T(8,128)(2,1)S(1)} all-to-all(bf16[64,18,128]{2,1,0:T(8,128)(2,1)S(1)} %reshape.66), channel_id=1, replica_groups=mesh['ep'=64,'tp'=8] {'ep'}, dimensions={0} | all-to-all | bytes 589824 | tf_op jit(solution)/shard_map/all_to_all | solution.py:45
  238.8 0.0 copy-done.1
  238.8 0.9 multiply_convert_fusion
  239.8 0.0 all-gather.2.cloned.1.call-update
  239.8 36.4 %all-gather.2.cloned.1.call-done = bf16[1152,1024]{1,0:T(8,128)(2,1)} async-done(((bf16[1152,128]{1,0:T(8,128)(2,1)}), bf16[1152,1024]{1,0:T(8,128)(2,1)}) %all-gather.2.cloned.1.call-update) | async-done | bytes 2359312 | tf_op jit(solution)/shard_map/all_gather | solution.py:63
  276.2 2.4 convolution_convert_fusion.2
  278.6 0.1 reshape.70
  278.8 3.9 %convolution_convert_fusion.1 = bf16[768,512]{1,0:T(8,128)(2,1)} fusion(bf16[1152,1024]{1,0:T(8,128)(2,1)} %all-gather.2.cloned.1.call-done, pred[]{:T(512)} %bitcast, bf16[2,512,1024]{2,1,0:T(8,128)(2,1)} %param.9), kind=kOutput, calls=%fused_computation.10 | convolution fusion | flops 806223872 | bytes 4456960 | tf_op jit(solution)/shard_map/dot_general | solution.py:77
  282.7 1.2 reshape.69
  283.9 1.6 pad_maximum_fusion.2
  285.5 15.4 %all-to-all-start.3 = ((bf16[64,18,512]{2,1,0:T(8,128)(2,1)}), bf16[64,18,512]{2,1,0:T(8,128)(2,1)S(1)}, u32[]{:S(2)}, u32[]{:S(2)}) async-start(bf16[64,18,512]{2,1,0:T(8,128)(2,1)} %pad_maximum_fusion.2), calls=%async_computation.4 | async-start | bytes 3145728 | tf_op jit(solution)/shard_map/all_to_all | solution.py:80
  300.9 13.2 %psum.7 = f32[128,8]{0,1:T(8,128)} all-reduce(f32[128,8]{0,1:T(8,128)S(1)} %get-tuple-element.4), channel_id=1, replica_groups=mesh['ep'=64,'tp'=8] {'tp'}, use_global_device_ids=true, to_apply=%region_7.8 | all-reduce | flops 1024 | bytes 8192 | tf_op jit(solution)/shard_map/psum | solution.py:75
  314.1 1.4 convolution_convert_fusion.5
  315.5 0.0 copy-start.3
  315.5 2.5 fusion.1
  318.0 0.0 copy-done.3
  318.0 1.9 fusion.4
  319.9 1.5 pad_maximum_fusion.1
  321.4 50.6 %all-to-all-done.3 = bf16[64,18,512]{2,1,0:T(8,128)(2,1)S(1)} async-done(((bf16[64,18,512]{2,1,0:T(8,128)(2,1)}), bf16[64,18,512]{2,1,0:T(8,128)(2,1)S(1)}, u32[]{:S(2)}, u32[]{:S(2)}) %all-to-all-start.3) | async-done | bytes 1179680 | tf_op jit(solution)/shard_map/all_to_all | solution.py:80
  372.0 0.4 reshape.71
  372.4 1.0 convolution_convert_fusion.3
  (9 shorter events, 0.3 us)
Async XLA Ops:
  7.2 8.6 %copy-start = (bf16[128,512]{1,0:T(8,128)(2,1)S(1)}, bf16[128,512]{1,0:T(8,128)(2,1)}, u32[]{:S(2)}) copy-start(bf16[128,512]{1,0:T(8,128)(2,1)} %param.6) | copy-start | bytes 393220
  17.6 19.5 %copy-start.6 = (s32[128]{0:T(128)S(1)}, s32[128]{0:T(128)}, u32[]{:S(2)}) copy-start(s32[128]{0:T(128)} %param.10) | copy-start | bytes 1540
  17.6 89.7 %all-to-all-start = ((bf16[64,18,512]{2,1,0:T(8,128)(2,1)}), bf16[64,18,512]{2,1,0:T(8,128)(2,1)S(1)}, u32[]{:S(2)}, u32[]{:S(2)}) async-start(bf16[64,18,512]{2,1,0:T(8,128)(2,1)} %reshape.61), calls=%async_computation | async-start | bytes 3145728 | tf_op jit(solution)/shard_map/all_to_all | solution.py:42
  37.0 123.0 %reduce-scatter.2.cloned.1.call-start = ((), (), s32[]{:S(2)}) async-start(), calls=%async_computation.5 | async-start | bytes 5308416 | tf_op jit(solution)/shard_map/reduce_scatter | solution.py:50
  110.8 2.4 copy-start.2
  116.7 159.5 %all-gather.2.cloned.1.call-start = ((), (), s32[]{:S(2)}) async-start(), calls=%async_computation.6 | async-start | bytes 2654208 | tf_op jit(solution)/shard_map/all_gather | solution.py:63
  161.2 35.9 %copy-start.4 = (bf16[128,128]{1,0:T(8,128)(2,1)S(1)}, bf16[128,128]{1,0:T(8,128)(2,1)}, u32[]{:S(2)}) copy-start(bf16[128,128]{1,0:T(8,128)(2,1)} %param.11) | copy-start | bytes 98308
  161.3 36.3 %copy-start.5 = (f32[128,8]{0,1:T(8,128)S(1)}, f32[128,8]{0,1:T(8,128)}, u32[]{:S(2)}) copy-start(f32[128,8]{0,1:T(8,128)} %param.8) | copy-start | bytes 12292
  197.6 41.3 %copy-start.1 = (f32[1152,128]{1,0:T(8,128)S(1)}, f32[1152,128]{1,0:T(8,128)}, u32[]{:S(2)}) copy-start(f32[1152,128]{1,0:T(8,128)} %reduce-scatter.2.cloned.1.call-done) | copy-start | bytes 1769476
  285.5 86.5 %all-to-all-start.3 = ((bf16[64,18,512]{2,1,0:T(8,128)(2,1)}), bf16[64,18,512]{2,1,0:T(8,128)(2,1)S(1)}, u32[]{:S(2)}, u32[]{:S(2)}) async-start(bf16[64,18,512]{2,1,0:T(8,128)(2,1)} %pad_maximum_fusion.2), calls=%async_computation.4 | async-start | bytes 3145728 | tf_op jit(solution)/shard_map/all_to_all | solution.py:80
  315.5 2.5 copy-start.3
Sparse Core Ops, SparseCore 0:
  116.9 43.1 reduce-scatter.1
  239.9 36.2 all-gather.1

commit v2 on v1

v2 whole, which is shorter than its diff:
```python
import functools

import jax
import jax.numpy as jnp
from jax import lax
from jax.experimental import pallas as pl
from jax.experimental.pallas import tpu as pltpu
from jax.sharding import PartitionSpec as P

MESH = pl.DeviceIdType.MESH
CAP = 6
CAPS = (2 * CAP, CAP)
NY = 4
BF16, F32 = jnp.bfloat16, jnp.float32


def dot(a, b, ca=1, cb=0):
    return lax.dot_general(a, b, (((ca,), (cb,)), ((), ())), preferred_element_type=F32)


def two_parts(value):
    high = value.astype(BF16)
    return high, (value - high.astype(F32)).astype(BF16)


def kernel(
    dims,
    info_ref, eid_ref, hot_ref, tokens_ref, grad_ref, weight_hbm,
    mixed_ref, gtok_ref, ggate_ref, gup_hbm,
    ring, inf, wraw, wsel, pmat, gatec, graw, xsend, xin, part, pin, psend, precv,
    act, aret, hgown, hg, brow, rret, ptok, rs, pmix, ms, pgg, gs, gup, gx,
    wsem, osem, lsem, ag, agi, ysem, csem, xsem, asem, hxsem, hcsem, bsem, rsem, msem, gsem, txsem,
):
    ny, nz, nx, topk = dims
    count, feat = tokens_ref.shape
    share = grad_ref.shape[1]
    ff = wsel.shape[2]
    half = nz // 2
    off = nz // 4 - 1
    nslot = nz // 2
    hrow, crow = CAPS[0] * nslot, CAPS[1] * nslot
    spans = [
        (j, h, (j * hrow if h == 0 else ny * hrow + j * crow), (hrow, crow)[h])
        for h in range(2)
        for j in range(ny)
    ]
    whole = [(0, ny * hrow), (ny * hrow, ny * crow)]
    rows = ny * (hrow + crow)
    t2 = count // 2

    ep, tp = lax.axis_index("ep"), lax.axis_index("tp")
    y, z = lax.div(ep, nz), lax.rem(ep, nz)
    x, c = lax.div(tp, 2), lax.rem(tp, 2)

    def device(yy, zz, xx, cc):
        return (lax.rem(yy, ny) * nz + lax.rem(zz, nz), lax.rem(xx, nx) * 2 + cc)

    z_to = (device(y, z + nz - 1, x, c), device(y, z + 1, x, c))
    y_to = [device(y + j, z, x, c) for j in range(ny)]
    y_back = [device(y + ny - j, z, x, c) for j in range(ny)]
    x_to = [device(y, z, x + i, c) for i in range(nx)]
    other = device(y, z, x, 1 - c)

    def pos(d):
        return (d + off) % nz

    def send(src, dst, sems, to):
        return pltpu.make_async_remote_copy(
            src_ref=src, dst_ref=dst, send_sem=sems.at[0], recv_sem=sems.at[1],
            device_id=to, device_id_type=MESH,
        )

    load = pltpu.make_async_copy(weight_hbm, wraw, wsem)
    load.start()
    barrier = pltpu.get_barrier_semaphore()
    partners = list(z_to) + y_to[1:] + x_to[1:] + [other]
    for partner in partners:
        pl.semaphore_signal(barrier, inc=1, device_id=partner, device_id_type=MESH)
    pl.semaphore_wait(barrier, len(partners))

    mine = pos(0) * count
    ring[mine : mine + count, :feat] = tokens_ref[...]
    ring[mine : mine + count, feat:] = grad_ref[...]
    inf[pos(0)] = info_ref[...]

    sign = (1, -1)

    def ag_copy(way, s, h):
        src, dst = pos(sign[way] * (s - 1)), pos(sign[way] * s)
        return send(
            ring.at[pl.ds(src * count + h * t2, t2)], ring.at[pl.ds(dst * count + h * t2, t2)],
            ag.at[way, s - 1, h], z_to[way],
        )

    def ag_info(way, s):
        src, dst = pos(sign[way] * (s - 1)), pos(sign[way] * s)
        return send(inf.at[src], inf.at[dst], agi.at[way, s - 1], z_to[way])

    def ag_has(way, s, h):
        return s < half or (s == half and h == way)

    def ag_info_has(way, s):
        return s < half or (s == half and way == 0)

    upper = (
        lax.broadcasted_iota(jnp.int32, (count, count), 0)
        < lax.broadcasted_iota(jnp.int32, (count, count), 1)
    ).astype(BF16)

    def y_copy(b, k, sems, src, dst, to):
        j, h, r0, n = spans[k]
        return send(src.at[b, pl.ds(r0, n)], dst.at[b, pl.ds(r0, n)], sems.at[b, k], to[j])

    def y_copies(b, sems, src, dst, to):
        return [y_copy(b, k, sems, src, dst, to) for k in range(len(spans)) if spans[k][0] > 0]

    def gather(b):
        eids = eid_ref[...]
        caps = jnp.where(lax.broadcasted_iota(jnp.int32, eids.shape, 0) % 2 == 0, CAPS[0], CAPS[1])
        caps = caps.astype(F32)
        names, gate_of = [], []
        for g in range(nslot):
            named = jnp.zeros(eids.shape, F32)
            gated = jnp.zeros(eids.shape, F32)
            block = inf[b * nslot + g]
            for k in range(topk):
                hit = block[k : k + 1] == eids
                named = named + jnp.where(hit, 1.0, 0.0)
                gated = gated + jnp.where(hit, block[topk + k : topk + k + 1], 0.0)
            names.append(named)
            gate_of.append(gated)
        rank = dot(jnp.concatenate(names, 0).astype(BF16), upper)
        place = []
        for g in range(nslot):
            r = rank[g * 2 * ny : (g + 1) * 2 * ny]
            place.append(jnp.where((names[g] > 0.0) & (r < caps), r + g * caps, -1.0))
        place = jnp.concatenate(place, 1)
        gate_of = jnp.concatenate(gate_of, 1)
        for j, h, r0, n in spans:
            e = 2 * j + h
            at = lax.broadcasted_iota(jnp.int32, (n, nslot * count), 0).astype(F32)
            hit = at == place[e : e + 1]
            pmat[b, r0 : r0 + n] = jnp.where(hit, 1.0, 0.0).astype(BF16)
            gate = jnp.sum(jnp.where(hit, gate_of[e : e + 1], 0.0), 1, keepdims=True)
            gatec[b, r0 : r0 + n] = jnp.broadcast_to(gate, (n, share))
        pick = pmat[b]
        base = b * nslot * count
        for c0 in range(0, feat, min(256, feat)):
            cols = slice(c0, c0 + min(256, feat))
            got = dot(pick, ring[base : base + nslot * count, cols]).astype(BF16)
            xsend[b, :, cols] = got
            xin[b, 0:hrow, cols] = got[0:hrow]
            xin[b, ny * hrow : ny * hrow + crow, cols] = got[ny * hrow : ny * hrow + crow]
        got = dot(pick, ring[base : base + nslot * count, feat:])
        graw[b] = got.astype(BF16)
        row_grad = (gatec[b] * got).astype(BF16)
        xsend[b, :, feat:] = row_grad
        xin[b, 0:hrow, feat:] = row_grad[0:hrow]
        xin[b, ny * hrow : ny * hrow + crow, feat:] = row_grad[ny * hrow : ny * hrow + crow]
        for copy in y_copies(b, ysem, xsend, xin, y_to):
            copy.start()

    def core_copy(b):
        return send(part.at[b, 1 - c], pin.at[b], csem.at[b], other)

    def forward(b):
        for copy in y_copies(b, ysem, xsend, xin, y_to):
            copy.wait_recv()
        for h, (r0, n) in enumerate(whole):
            rows_in = xin[b, r0 : r0 + n, :feat]
            for t in range(0, ff // share, 2):
                out = dot(rows_in, wsel[h, :, t * share : (t + 2) * share]).astype(BF16)
                part[b, 0, t // 2, r0 : r0 + n] = out[:, :share]
                part[b, 1, t // 2, r0 : r0 + n] = out[:, share:]
        core_copy(b).start()

    def x_copy(b, i):
        return send(psend.at[b, i], precv.at[b, i], xsem.at[b, i], x_to[i])

    def pair_sum(b):
        core_copy(b).wait_recv()
        for i in [*range(1, nx), 0]:
            to = lax.rem(x + i, nx)
            total = part[b, c, to].astype(F32) + pin[b, to].astype(F32)
            psend[b, i] = total.astype(BF16)
            if i > 0:
                x_copy(b, i).start()

    def strip(b, t):
        return hg.at[b, :, pl.ds(pl.multiple_of(t * share, share), share)]

    def hg_x(b, i):
        return send(hgown.at[b], strip(b, tp), hxsem.at[b, i], x_to[i])

    def hg_core(b, i):
        t = lax.rem(x + nx - i, nx) * 2 + c
        return send(hgown.at[b] if i == 0 else strip(b, t), strip(b, t), hcsem.at[b, i], other)

    def hg_keep(b):
        return pltpu.make_async_copy(hgown.at[b], strip(b, tp), lsem.at[b])

    def middle(b):
        hidden = psend[b, 0].astype(F32)
        for i in range(1, nx):
            x_copy(b, i).wait_recv()
            hidden = hidden + precv[b, i].astype(F32)
        sig = jax.nn.sigmoid(hidden)
        row_grad = xin[b, :, feat:].astype(F32)
        hgown[b] = (row_grad * (sig * (1.0 + hidden * (1.0 - sig)))).astype(BF16)
        for i in range(1, nx):
            hg_x(b, i).start()
        hg_core(b, 0).start()
        hg_keep(b).start()
        acts = (hidden * sig).astype(BF16)
        act[b] = acts
        aret[b, 0:hrow] = acts[0:hrow]
        aret[b, ny * hrow : ny * hrow + crow] = acts[ny * hrow : ny * hrow + crow]
        for copy in y_copies(b, asem, act, aret, y_back):
            copy.start()

    def hg_forward(b):
        for i in range(1, nx):
            hg_x(b, i).wait_recv()
            hg_core(b, i).start()

    def mix(b):
        for copy in y_copies(b, asem, act, aret, y_back):
            copy.wait_recv()
        acts = aret[b].astype(F32)
        base = b * nslot * count
        weighted = (gatec[b] * acts).astype(BF16)
        pmix[base : base + nslot * count] = dot(pmat[b], weighted, 0, 0).astype(BF16)
        high, low = two_parts(acts * graw[b].astype(F32))
        ones = jnp.ones((8, share), BF16)
        sums = []
        for j, h, r0, n in spans:
            line = dot(ones, high[r0 : r0 + n], 1, 1) + dot(ones, low[r0 : r0 + n], 1, 1)
            line_high, line_low = two_parts(line)
            spread = pmat[b, r0 : r0 + n]
            sums.append((2 * j + h, dot(line_high, spread) + dot(line_low, spread)))
        for g in range(nslot):
            named = inf[b * nslot + g, :topk]
            out = jnp.zeros((topk, count), F32)
            for e, value in sums:
                here = value[:topk, g * count : (g + 1) * count]
                out = out + jnp.where(named == eid_ref[e : e + 1], here, 0.0)
            pgg[b * nslot + g] = out

    def backward(b):
        hg_keep(b).wait()
        for i in range(nx):
            hg_core(b, i).wait_recv()
        for h, (r0, n) in enumerate(whole):
            out = dot(hg[b, r0 : r0 + n], wsel[h], 1, 1).astype(BF16)
            brow[b, r0 : r0 + n] = out
            own = (hrow, crow)[h]
            rret[b, r0 : r0 + own] = out[0:own]
        for copy in y_copies(b, bsem, brow, rret, y_back):
            copy.start()

    def scatter(b):
        for copy in y_copies(b, bsem, brow, rret, y_back):
            copy.wait_recv()
        base = b * nslot * count
        ptok[base : base + nslot * count] = dot(pmat[b], rret[b], 0, 0).astype(BF16)

    def weight_grad(k):
        wide = ff // 4
        cols = slice(k * wide, (k + 1) * wide)
        sums = []
        for r0, n in whole:
            total = dot(xin[0, r0 : r0 + n, :feat], hg[0, r0 : r0 + n, cols], 0, 0)
            sums.append(total + dot(xin[1, r0 : r0 + n, :feat], hg[1, r0 : r0 + n, cols], 0, 0))
        swap = hot_ref[:, cols] > 0.0
        gup[0, :, cols] = jnp.where(swap, sums[1], sums[0]).astype(BF16)
        gup[1, :, cols] = jnp.where(swap, sums[0], sums[1]).astype(BF16)

    def rs_copy(way, d, h):
        src = pos(sign[1 - way] * d) * count + h * t2
        return send(
            ptok.at[pl.ds(src, t2)], rs.at[way, d - 1, pl.ds(h * t2, t2)],
            rsem.at[way, d - 1, h], z_to[way],
        )

    def rs_has(way, d, h):
        return d < half or (d == half and h == 1 - way)

    def rs_start(d):
        for way, h in ((1, 0), (0, 1), (1, 1), (0, 0)):
            if d == half and not rs_has(way, d, h):
                continue
            if rs_has(way, d + 1, h) and d < half:
                continue
            rs_copy(way, d, h).start()

    def rs_step(d):
        for h in range(2):
            for way in (1, 0):
                if not rs_has(way, d + 1, h):
                    continue
                rs_copy(way, d + 1, h).wait_recv()
                at = pos(sign[1 - way] * d) * count + h * t2
                arrived = rs[way, d, h * t2 : (h + 1) * t2].astype(F32)
                ptok[at : at + t2] = (ptok[at : at + t2].astype(F32) + arrived).astype(BF16)
                rs_copy(way, d, h).start()

    def rs_end():
        for h in range(2):
            total = ptok[mine + h * t2 : mine + (h + 1) * t2].astype(F32)
            for way in (1, 0):
                rs_copy(way, 1, h).wait_recv()
                total = total + rs[way, 0, h * t2 : (h + 1) * t2].astype(F32)
            gtok_ref[h * t2 : (h + 1) * t2] = total.astype(BF16)

    def ms_copy(way, d):
        src = pos(sign[1 - way] * d)
        return send(
            pmix.at[pl.ds(src * count, count)], ms.at[way, d - 1], msem.at[way, d - 1], z_to[way]
        )

    def gs_copy(way, d):
        src = pos(sign[1 - way] * d)
        return send(pgg.at[src], gs.at[way, d - 1], gsem.at[way, d - 1], z_to[way])

    def ms_has(way, d):
        return d < half or (d == half and way == 1)

    def ms_step(d):
        for way in (1, 0):
            if not ms_has(way, d):
                continue
            if ms_has(way, d + 1):
                src = pos(sign[1 - way] * d)
                ms_copy(way, d + 1).wait_recv()
                at = slice(src * count, (src + 1) * count)
                pmix[at] = (pmix[at].astype(F32) + ms[way, d].astype(F32)).astype(BF16)
                gs_copy(way, d + 1).wait_recv()
                pgg[src] = pgg[src] + gs[way, d]
            ms_copy(way, d).start()
            gs_copy(way, d).start()

    def tx_core():
        return send(gx.at[0], gx.at[1], txsem.at[0], other)

    def tx_copy(i):
        return send(gx.at[2], gx.at[2 + i], txsem.at[i], x_to[i])

    def ms_end():
        total = pmix[mine : mine + count].astype(F32)
        gates = pgg[pos(0)]
        for way in (1, 0):
            ms_copy(way, 1).wait_recv()
            total = total + ms[way, 0].astype(F32)
            gs_copy(way, 1).wait_recv()
            gates = gates + gs[way, 0]
        mixed_ref[...] = total.astype(BF16)
        gx[0] = gates
        tx_core().start()

    def tx_middle():
        tx_core().wait_recv()
        gx[2] = gx[0] + gx[1]
        for i in range(1, nx):
            tx_copy(i).start()

    def tx_end():
        total = gx[2]
        for i in range(1, nx):
            tx_copy(i).wait_recv()
            total = total + gx[2 + i]
        ggate_ref[...] = total

    def order_weights():
        load.wait()
        for k in range(4):
            cols = slice(k * (ff // 4), (k + 1) * (ff // 4))
            swap = hot_ref[:, cols] > 0.0
            first, second = wraw[0, :, cols].astype(F32), wraw[1, :, cols].astype(F32)
            wsel[0, :, cols] = jnp.where(swap, second, first).astype(BF16)
            wsel[1, :, cols] = jnp.where(swap, first, second).astype(BF16)

    for way in (0, 1):
        ag_info(way, 1).start()
    for h in range(2):
        for way in (0, 1):
            ag_copy(way, 1, h).start()
    early = [order_weights]
    ready = nz // 4
    stages = [
        functools.partial(gather, 0), functools.partial(forward, 0),
        functools.partial(pair_sum, 0), functools.partial(middle, 0),
        functools.partial(hg_forward, 0), functools.partial(mix, 0),
        functools.partial(backward, 0), functools.partial(scatter, 0),
    ]
    done = 0
    for s in range(1, half + 1):
        for way in (0, 1):
            if ag_info_has(way, s):
                ag_info(way, s).wait_recv()
                if ag_info_has(way, s + 1):
                    ag_info(way, s + 1).start()
        for h in range(2):
            for way in (0, 1):
                if ag_has(way, s, h):
                    ag_copy(way, s, h).wait_recv()
                    if ag_has(way, s + 1, h):
                        ag_copy(way, s + 1, h).start()
        if s == 1:
            order_weights()
        if ready <= s < half:
            stages[done]()
            done += 1
    late = [
        functools.partial(gather, 1), functools.partial(forward, 1),
        functools.partial(pair_sum, 1), functools.partial(middle, 1),
    ]
    for stage in late:
        stage()
        if done < len(stages):
            stages[done]()
            done += 1
    while done < len(stages):
        stages[done]()
        done += 1
    hg_forward(1)
    mix(1)
    steps = list(range(half, 0, -1))
    for d in steps[:2]:
        ms_step(d)
    backward(1)
    for d in steps[2:5]:
        ms_step(d)
    scatter(1)
    rest = [functools.partial(ms_step, d) for d in steps[5:]] + [ms_end, tx_middle, tx_end]
    rest = rest + [functools.partial(weight_grad, k) for k in range(4)]
    rs_start(half)
    if half > 1:
        rs_start(half - 1)
    for d in range(half - 1, 0, -1):
        rs_step(d)
        for _ in range(2):
            if rest:
                rest.pop(0)()
    for job in rest:
        job()
    store = pltpu.make_async_copy(gup, gup_hbm, osem)
    store.start()
    rs_end()
    store.wait()

    for s in range(1, half + 1):
        for way in (0, 1):
            if ag_info_has(way, s):
                ag_info(way, s).wait_send()
            for h in range(2):
                if ag_has(way, s, h):
                    ag_copy(way, s, h).wait_send()
                if rs_has(way, s, h):
                    rs_copy(way, s, h).wait_send()
            if ms_has(way, s):
                ms_copy(way, s).wait_send()
                gs_copy(way, s).wait_send()
    for b in range(2):
        for copy in y_copies(b, ysem, xsend, xin, y_to):
            copy.wait_send()
        for copy in y_copies(b, asem, act, aret, y_back):
            copy.wait_send()
        for copy in y_copies(b, bsem, brow, rret, y_back):
            copy.wait_send()
        core_copy(b).wait_send()
        for i in range(nx):
            hg_core(b, i).wait_send()
            if i > 0:
                x_copy(b, i).wait_send()
                hg_x(b, i).wait_send()
    tx_core().wait_send()
    for i in range(1, nx):
        tx_copy(i).wait_send()


def on_device(ny, tokens, routes, gates, up_weight, replica_on, grad_out):
    count, feat = tokens.shape
    topk = routes.shape[1]
    share = grad_out.shape[1]
    ff = up_weight.shape[2]
    experts = replica_on.shape[0]
    nz = lax.axis_size("ep") // ny
    nx = lax.axis_size("tp") // 2
    me = lax.axis_index("ep")
    info = jnp.concatenate([routes.T.astype(F32), gates.T], 0)
    line = jnp.arange(2 * ny, dtype=jnp.int32)
    home = ((me // nz + line // 2) % ny) * nz + me % nz
    second = jnp.arange(experts, dtype=jnp.int32)[None, :] == (2 * home + 1)[:, None]
    second = jnp.sum(jnp.where(second, replica_on[None, :], 0), 1)
    eids = 2 * home + jnp.where(line % 2 == 0, second, 1 - second)
    eids = jnp.broadcast_to(eids.astype(F32)[:, None], (2 * ny, count))
    hot = jnp.broadcast_to(second[0].astype(F32), (1, ff))

    half = nz // 2
    rows = ny * half * 3 * CAP
    slots = half * count
    vmem = pl.BlockSpec(memory_space=pltpu.VMEM)
    hbm = pl.BlockSpec(memory_space=pl.ANY)

    def dma(*shape):
        return pltpu.SemaphoreType.DMA(shape + (2,))

    mixed, gtok, ggate, gup = pl.pallas_call(
        functools.partial(kernel, (ny, nz, nx, topk)),
        out_shape=[
            jax.ShapeDtypeStruct((count, share), BF16),
            jax.ShapeDtypeStruct((count, feat), BF16),
            jax.ShapeDtypeStruct((topk, count), F32),
            jax.ShapeDtypeStruct(up_weight.shape, BF16),
        ],
        in_specs=[vmem] * 5 + [hbm],
        out_specs=[vmem] * 3 + [hbm],
        scratch_shapes=[
            pltpu.VMEM((nz * count, feat + share), BF16),
            pltpu.VMEM((nz, 2 * topk, count), F32),
            pltpu.VMEM(up_weight.shape, BF16),
            pltpu.VMEM(up_weight.shape, BF16),
            pltpu.VMEM((2, rows, slots), BF16),
            pltpu.VMEM((2, rows, share), F32),
            pltpu.VMEM((2, rows, share), BF16),
            pltpu.VMEM((2, rows, feat + share), BF16),
            pltpu.VMEM((2, rows, feat + share), BF16),
            pltpu.VMEM((2, 2, nx, rows, share), BF16),
            pltpu.VMEM((2, nx, rows, share), BF16),
            pltpu.VMEM((2, nx, rows, share), BF16),
            pltpu.VMEM((2, nx, rows, share), BF16),
            pltpu.VMEM((2, rows, share), BF16),
            pltpu.VMEM((2, rows, share), BF16),
            pltpu.VMEM((2, rows, share), BF16),
            pltpu.VMEM((2, rows, ff), BF16),
            pltpu.VMEM((2, rows, feat), BF16),
            pltpu.VMEM((2, rows, feat), BF16),
            pltpu.VMEM((nz * count, feat), BF16),
            pltpu.VMEM((2, half, count, feat), BF16),
            pltpu.VMEM((nz * count, share), BF16),
            pltpu.VMEM((2, half, count, share), BF16),
            pltpu.VMEM((nz, topk, count), F32),
            pltpu.VMEM((2, half, topk, count), F32),
            pltpu.VMEM(up_weight.shape, BF16),
            pltpu.VMEM((2 + nx, topk, count), F32),
            pltpu.SemaphoreType.DMA,
            pltpu.SemaphoreType.DMA,
            pltpu.SemaphoreType.DMA((2,)),
            dma(2, half, 2),
            dma(2, half),
            dma(2, 2 * ny),
            dma(2),
            dma(2, nx),
            dma(2, 2 * ny),
            dma(2, nx),
            dma(2, nx),
            dma(2, 2 * ny),
            dma(2, half, 2),
            dma(2, half),
            dma(2, half),
            dma(nx),
        ],
        compiler_params=pltpu.CompilerParams(
            collective_id=0, has_side_effects=True, vmem_limit_bytes=56 * 1024 * 1024
        ),
        cost_estimate=pl.CostEstimate(
            flops=8 * rows * feat * ff, bytes_accessed=8 * feat * ff, transcendentals=2 * rows * share
        ),
    )(info, eids, hot, tokens, grad_out, up_weight)
    return mixed, gtok, ggate.T, gup


def solution(mesh, ny=NY):
    return jax.shard_map(
        functools.partial(on_device, ny),
        mesh=mesh,
        in_specs=(
            P("ep", "tp"), P("ep", None), P("ep", None), P("ep", "tp", None), P(), P("ep", "tp"),
        ),
        out_specs=(P("ep", "tp"), P("ep", "tp"), P("ep", None), P("ep", "tp", None)),
        check_vma=False,
    )
```

time: 385 us -> 154 us (0.40)
  waiting for transfers between devices: 199 us -> 0 us
  Pallas kernels: 0 us -> 141 us
  blocking collectives: 80 us -> 0 us
  starting transfers between devices: 34.9 us -> 0 us
  other arithmetic: 25.1 us -> 2.85 us
  matrix products: 17.5 us -> 0 us
  between operations: 15 us -> 0.72 us
    pallas_call x0 -> x1, Pallas kernels: none -> 141 us  [on_device(): pl.pallas_call(functools.partial(kernel, (ny, nz, nx, topk)), out_shape=[...]
    all_to_all x2 -> x0, waiting for transfers between devices: 120 us -> none  [the longest x1 69 us: on_device(): lax.all_to_all(sent, 'ep', split_axis=0, concat_axis=0, tiled=True)]
    all_to_all x2 -> x0, blocking collectives: 66.8 us -> none  [the longest x1 35.5 us: on_device(): lax.all_to_all(by_group(act), 'ep', split_axis=0, concat_axis=0, tiled=True)]
    reduce_scatter x1 -> x0, waiting for transfers between devices: 43.2 us -> none  [on_device(): lax.psum_scatter(partial_value, 'tp', scatter_dimension=1, tiled=True)]
    all_gather x1 -> x0, waiting for transfers between devices: 36.4 us -> none  [on_device(): hidden_grad = lax.all_gather(grad_part, 'tp', axis=1, tiled=True)]
    all_to_all x2 -> x0, starting transfers between devices: 34.8 us -> none  [the longest x1 19.4 us: on_device(): lax.all_to_all(sent, 'ep', split_axis=0, concat_axis=0, tiled=True)]
    dot_general x11 -> x0, matrix products: 17.5 us -> none  [the longest x5 4.44 us: exact_dot(): return jnp.dot(a, b, preferred_element_type=jnp.float32)]
    psum x1 -> x0, blocking collectives: 13.2 us -> none  [on_device(): grad_gates = lax.psum(gate_pairs, 'tp')]
  transfers between devices with their start and end apart: 4 -> 0, of which waited for: 4 -> 0; matrix products, arithmetic and copies ran while one was open for 2% -> 0% of each run, Pallas kernels for 0% -> 0%
where the time goes in v2:
time: 154 us; the launch traced here: 153 us
  Pallas kernels  141 us (92%)
  local copies, waits for them, and re-layouts  8.55 us (6%)
  other arithmetic  2.85 us (2%)
    pallas_call x1, Pallas kernels, on_device(): pl.pallas_call(functools.partial(kernel, (ny, nz, nx, topk)), out_shape=[...  141 us
    unnamed x4, local copies, waits for them, and re-layouts  7.29 us

profile of v2, /device:TPU:1, one launch (start us, length us, event | category | flops | bytes accessed | tf_op | source)
XLA Modules:
  0.0 153.0 jit_solution(14122394350418889629)
XLA Ops:
  0.7 0.8 select_reduce_fusion
  1.6 0.7 broadcast_in_dim.26.eid_ref
  2.2 0.6 broadcast_in_dim.27.hot_ref
  2.8 0.7 convert_bitcast_fusion
  3.5 1.3 pad_maximum_fusion.info_ref
  4.8 140.9 %shard_map.93 = (bf16[128,128]{1,0:T(8,128)(2,1)}, bf16[128,512]{1,0:T(8,128)(2,1)}, f32[8,128]{1,0:T(8,128)}, bf16[2,512,1024]{2,1,0:T(8,128)(2,1)}) custom-call(f32[16,128]{1,0:T(8,128)} %pad_maximum_fusion.info_ref, f32[8,128]{1,0:T(8,128)} %broadcast_in_dim.26.eid_ref, f32[1,1024]{1,0:T(1,128)} %broadcast_in_dim.27.hot_ref, bf16[128,512]{1,0:T(8,128)(2,1)} %tokens_ref.1, ...), custom_call_target="tpu_custom_call" | custom-call | flops 2415919104 | bytes 4194304 | tf_op jit(solution)/shard_map/pallas_call | solution.py:508
  145.7 1.4 copy.14
  147.0 1.6 %copy.15 = bf16[128,512]{1,0:T(8,128)(2,1)} copy(bf16[128,512]{1,0:T(8,128)(2,1)} %get-tuple-element.17) | data formatting | bytes 262144
  148.6 1.3 copy.16
  149.9 3.1 %copy.17 = bf16[2,512,1024]{2,1,0:T(8,128)(2,1)} copy(bf16[2,512,1024]{2,1,0:T(8,128)(2,1)} %get-tuple-element.19) | data formatting | bytes 4194304
  (2 shorter events, 0.0 us)

commit v3 on v2

v3 whole, which is shorter than its diff:
```python
import functools

import jax
import jax.numpy as jnp
from jax import lax
from jax.experimental import pallas as pl
from jax.experimental.pallas import tpu as pltpu
from jax.sharding import PartitionSpec as P

MESH = pl.DeviceIdType.MESH
CAP = 6
CAPS = (2 * CAP, CAP)
NY = 4
PIECES = 8
SIZES = (4, 4, 4, 2, 2)
BATCHES = len(SIZES)
BF16, F32 = jnp.bfloat16, jnp.float32


def dot(a, b, ca=1, cb=0):
    return lax.dot_general(a, b, (((ca,), (cb,)), ((), ())), preferred_element_type=F32)


def two_parts(value):
    high = value.astype(BF16)
    return high, (value - high.astype(F32)).astype(BF16)


def slot_order(nz):
    order = [0]
    for far in range(1, nz // 2):
        order += [far, nz - far]
    return order + [nz // 2]


def block_rows(nslot):
    return tuple(-(-cap * nslot // 16) * 16 for cap in CAPS)


DURING = {
    (2, 3): "g0", (4, 2): "f0", (4, 3): "g1", (5, 0): "p0", (6, 1): "m0", (6, 2): "f1",
    (6, 3): "g2", (7, 0): "p1", (7, 2): "h0", (7, 3): "g3", (8, 0): "b0", (8, 1): "m1 f2",
    (8, 3): "g4",
}
BETWEEN = (
    "p2 f3 x0 p3 s0 f4 h1 x1 p4 m2 m3 b1 m4 h2 x2 x3 h3 b2 b3 s1 x4 M8 h4 M7 b4 M6 s3 M5 s4"
)


def kernel(
    dims,
    routes_ref, gates_ref, rep_ref, tokens_ref, grad_ref, weight_hbm,
    mixed_ref, gtok_ref, ggate_ref, gup_hbm,
    eid, hot, ring, inf, wraw, wsel, pmat, gatec, graw, xsend, xin, part, pin, psend, precv,
    act, aret, hgown, hg, brow, rret, ptok, rs, pmix, ms, pgg, gs, gup, gx,
    wsem, osem, lsem, ag, agi, ysem, csem, xsem, asem, hxsem, hcsem, bsem, rsem, msem, gsem, txsem,
):
    ny, nz, nx = dims
    count, feat = tokens_ref.shape
    topk = routes_ref.shape[0]
    experts = rep_ref.shape[1]
    share = grad_ref.shape[1]
    ff = wsel.shape[2]
    half = nz // 2
    order = slot_order(nz)
    first_slot = [sum(SIZES[:b]) for b in range(BATCHES)]
    pads = [block_rows(size) for size in SIZES]
    blocks_of = [sum(pad) for pad in pads]
    rows_of = [ny * block for block in blocks_of]

    def spans(b):
        return [
            (j, h, j * blocks_of[b] + h * pads[b][0], pads[b][h]) for j in range(ny) for h in range(2)
        ]

    def groups(b):
        return slice(first_slot[b] * count, (first_slot[b] + SIZES[b]) * count)

    quarter = count // 4

    ep, tp = lax.axis_index("ep"), lax.axis_index("tp")
    y, z = lax.div(ep, nz), lax.rem(ep, nz)
    x, c = lax.div(tp, 2), lax.rem(tp, 2)

    def device(yy, zz, xx, cc):
        return (lax.rem(yy, ny) * nz + lax.rem(zz, nz), lax.rem(xx, nx) * 2 + cc)

    z_to = (device(y, z + nz - 1, x, c), device(y, z + 1, x, c))
    y_to = [device(y + j, z, x, c) for j in range(ny)]
    y_back = [device(y + ny - j, z, x, c) for j in range(ny)]
    x_to = [device(y, z, x + i, c) for i in range(nx)]
    other = device(y, z, x, 1 - c)

    def pos(d):
        return order.index(d % nz)

    def send(src, dst, sems, to):
        return pltpu.make_async_remote_copy(
            src_ref=src, dst_ref=dst, send_sem=sems.at[0], recv_sem=sems.at[1],
            device_id=to, device_id_type=MESH,
        )

    load = pltpu.make_async_copy(weight_hbm, wraw, wsem)
    load.start()
    barrier = pltpu.get_barrier_semaphore()
    partners = list(z_to) + y_to[1:] + x_to[1:] + [other]
    for partner in partners:
        pl.semaphore_signal(barrier, inc=1, device_id=partner, device_id_type=MESH)

    mine = pos(0) * count
    ring[mine : mine + count, :feat] = tokens_ref[...]
    ring[mine : mine + count, feat:] = grad_ref[...]
    inf[pos(0), :topk] = routes_ref[...].astype(F32)
    inf[pos(0), topk:] = gates_ref[...]

    def homes(width):
        line = lax.broadcasted_iota(jnp.int32, (2 * ny, width), 0)
        return line, lax.rem(y + lax.shift_right_logical(line, 1), ny) * nz + z

    line, home = homes(experts)
    at = lax.broadcasted_iota(jnp.int32, (2 * ny, experts), 1) == 2 * home + 1
    second = jnp.sum(jnp.where(at, rep_ref[...].astype(F32), 0.0), 1, keepdims=True)
    line, home = homes(count)
    second = jnp.broadcast_to(second, (2 * ny, count))
    eid[...] = 2.0 * home.astype(F32) + jnp.where(lax.rem(line, 2) == 0, second, 1.0 - second)
    hot[...] = second

    def swap(shape):
        return jnp.broadcast_to(hot[0:1, 0:1], shape) > 0.0

    pl.semaphore_wait(barrier, len(partners))

    sign = (1, -1)

    def ag_copy(way, s, q):
        src, dst = pos(sign[way] * (s - 1)) * count, pos(sign[way] * s) * count
        return send(
            ring.at[pl.ds(src + q * quarter, quarter)], ring.at[pl.ds(dst + q * quarter, quarter)],
            ag.at[way, s - 1, q], z_to[way],
        )

    def ag_has(way, s, q):
        return s < half or (s == half and q // 2 == way)

    def ag_info(way, s):
        src, dst = pos(sign[way] * (s - 1)), pos(sign[way] * s)
        return send(inf.at[src], inf.at[dst], agi.at[way, s - 1], z_to[way])

    def ag_info_has(way, s):
        return s < half or (s == half and way == 0)

    def ag_start():
        for q in range(4):
            for way in (0, 1):
                ag_copy(way, 1, q).start()
                if q == 0:
                    ag_info(way, 1).start()

    def ag_step(s, q):
        for way in (0, 1):
            if ag_has(way, s, q):
                ag_copy(way, s, q).wait_recv()
                if ag_has(way, s + 1, q):
                    ag_copy(way, s + 1, q).start()
            if q == 0 and ag_info_has(way, s):
                ag_info(way, s).wait_recv()
                if ag_info_has(way, s + 1):
                    ag_info(way, s + 1).start()

    def blocks(ref, b, h, cols=slice(None)):
        return jnp.concatenate([ref[b, r0 : r0 + n, cols] for j, hh, r0, n in spans(b) if hh == h], 0)

    def y_copies(b, sems, src, dst, to):
        block = blocks_of[b]
        return [
            send(
                src.at[b, pl.ds(j * block, block)], dst.at[b, pl.ds(j * block, block)],
                sems.at[b, j], to[j],
            )
            for j in range(1, ny)
        ]

    def gather(b):
        nslot, rows, block = SIZES[b], rows_of[b], blocks_of[b]
        eids = eid[...]
        caps = lax.rem(lax.broadcasted_iota(jnp.int32, eids.shape, 0), 2) == 0
        caps = jnp.where(caps, float(CAPS[0]), float(CAPS[1]))
        names, gate_of = [], []
        for g in range(nslot):
            named = jnp.zeros(eids.shape, F32)
            gated = jnp.zeros(eids.shape, F32)
            routing = inf[first_slot[b] + g]
            for k in range(topk):
                hit = routing[k : k + 1] == eids
                named = named + jnp.where(hit, 1.0, 0.0)
                gated = gated + jnp.where(hit, routing[topk + k : topk + k + 1], 0.0)
            names.append(named)
            gate_of.append(gated)
        upper = (
            lax.broadcasted_iota(jnp.int32, (count, count), 0)
            < lax.broadcasted_iota(jnp.int32, (count, count), 1)
        ).astype(BF16)
        rank = dot(jnp.concatenate(names, 0).astype(BF16), upper)
        place = []
        for g in range(nslot):
            r = rank[g * 2 * ny : (g + 1) * 2 * ny]
            place.append(jnp.where((names[g] > 0.0) & (r < caps), r + g * caps, -1.0))
        place = jnp.concatenate(place, 1)
        gate_of = jnp.concatenate(gate_of, 1)
        for j, h, r0, n in spans(b):
            e = 2 * j + h
            row = lax.broadcasted_iota(jnp.int32, (n, nslot * count), 0).astype(F32)
            hit = row == place[e : e + 1]
            pmat[b, r0 : r0 + n, : nslot * count] = jnp.where(hit, 1.0, 0.0).astype(BF16)
            gate = jnp.sum(jnp.where(hit, gate_of[e : e + 1], 0.0), 1, keepdims=True)
            gatec[b, r0 : r0 + n] = jnp.broadcast_to(gate, (n, share))
        pick = pmat[b, :rows, : nslot * count]
        for c0 in range(0, feat, min(256, feat)):
            cols = slice(c0, c0 + min(256, feat))
            got = dot(pick, ring[groups(b), cols]).astype(BF16)
            xsend[b, :rows, cols] = got
            xin[b, 0:block, cols] = got[0:block]
        got = dot(pick, ring[groups(b), feat:])
        graw[b, :rows] = got.astype(BF16)
        row_grad = (gatec[b, :rows] * got).astype(BF16)
        xsend[b, :rows, feat:] = row_grad
        xin[b, 0:block, feat:] = row_grad[0:block]
        for copy in y_copies(b, ysem, xsend, xin, y_to):
            copy.start()

    def core_copy(b):
        rows = pl.ds(0, rows_of[b])
        return send(part.at[b, 1 - c, :, rows], pin.at[b, :, rows], csem.at[b], other)

    def forward(b):
        for copy in y_copies(b, ysem, xsend, xin, y_to):
            copy.wait_recv()
        for h in range(2):
            rows_in = blocks(xin, b, h, slice(0, feat))
            for t in range(0, ff // share, 2):
                out = dot(rows_in, wsel[h, :, t * share : (t + 2) * share]).astype(BF16)
                for j, hh, r0, n in spans(b):
                    if hh == h:
                        part[b, 0, t // 2, r0 : r0 + n] = out[j * n : (j + 1) * n, :share]
                        part[b, 1, t // 2, r0 : r0 + n] = out[j * n : (j + 1) * n, share:]
        core_copy(b).start()

    def x_copy(b, i):
        rows = pl.ds(0, rows_of[b])
        return send(psend.at[b, i, rows], precv.at[b, i, rows], xsem.at[b, i], x_to[i])

    def pair_sum(b):
        core_copy(b).wait_recv()
        for i in [*range(1, nx), 0]:
            to = lax.rem(x + i, nx)
            rows = slice(0, rows_of[b])
            total = part[b, c, to, rows].astype(F32) + pin[b, to, rows].astype(F32)
            psend[b, i, rows] = total.astype(BF16)
            if i > 0:
                x_copy(b, i).start()

    def strip(b, t):
        return hg.at[b, pl.ds(0, rows_of[b]), pl.ds(pl.multiple_of(t * share, share), share)]

    def own_strip(b):
        return hgown.at[b, pl.ds(0, rows_of[b])]

    def hg_x(b, i):
        return send(own_strip(b), strip(b, tp), hxsem.at[b, i], x_to[i])

    def hg_core(b, i):
        t = lax.rem(x + nx - i, nx) * 2 + c
        return send(own_strip(b) if i == 0 else strip(b, t), strip(b, t), hcsem.at[b, i], other)

    def hg_keep(b):
        return pltpu.make_async_copy(own_strip(b), strip(b, tp), lsem.at[b])

    def middle(b):
        rows, block = rows_of[b], blocks_of[b]
        hidden = psend[b, 0, :rows].astype(F32)
        for i in range(1, nx):
            x_copy(b, i).wait_recv()
            hidden = hidden + precv[b, i, :rows].astype(F32)
        sig = jax.nn.sigmoid(hidden)
        row_grad = xin[b, :rows, feat:].astype(F32)
        hgown[b, :rows] = (row_grad * (sig * (1.0 + hidden * (1.0 - sig)))).astype(BF16)
        for i in range(1, nx):
            hg_x(b, i).start()
        hg_core(b, 0).start()
        hg_keep(b).start()
        acts = (hidden * sig).astype(BF16)
        act[b, :rows] = acts
        aret[b, 0:block] = acts[0:block]
        for copy in y_copies(b, asem, act, aret, y_back):
            copy.start()

    def hg_forward(b):
        for i in range(1, nx):
            hg_x(b, i).wait_recv()
            hg_core(b, i).start()

    def mix(b):
        for copy in y_copies(b, asem, act, aret, y_back):
            copy.wait_recv()
        nslot, rows = SIZES[b], rows_of[b]
        acts = aret[b, :rows].astype(F32)
        weighted = (gatec[b, :rows] * acts).astype(BF16)
        pmix[groups(b)] = dot(pmat[b, :rows, : nslot * count], weighted, 0, 0).astype(BF16)
        high, low = two_parts(acts * graw[b, :rows].astype(F32))
        ones = jnp.ones((8, share), BF16)
        sums = []
        for j, h, r0, n in spans(b):
            line = dot(ones, high[r0 : r0 + n], 1, 1) + dot(ones, low[r0 : r0 + n], 1, 1)
            line_high, line_low = two_parts(line)
            spread = pmat[b, r0 : r0 + n, : nslot * count]
            sums.append((2 * j + h, dot(line_high, spread) + dot(line_low, spread)))
        for g in range(nslot):
            named = inf[first_slot[b] + g, :topk]
            out = jnp.zeros((topk, count), F32)
            for e, value in sums:
                here = value[:topk, g * count : (g + 1) * count]
                out = out + jnp.where(named == eid[e : e + 1], here, 0.0)
            pgg[first_slot[b] + g] = out

    def backward(b):
        hg_keep(b).wait()
        for i in range(nx):
            hg_core(b, i).wait_recv()
        for h in range(2):
            out = dot(blocks(hg, b, h), wsel[h], 1, 1).astype(BF16)
            for j, hh, r0, n in spans(b):
                if hh == h:
                    (rret if j == 0 else brow)[b, r0 : r0 + n] = out[j * n : (j + 1) * n]
        for copy in y_copies(b, bsem, brow, rret, y_back):
            copy.start()

    def scatter(b):
        for copy in y_copies(b, bsem, brow, rret, y_back):
            copy.wait_recv()
        rows = rows_of[b]
        pick = pmat[b, :rows, : SIZES[b] * count]
        ptok[groups(b)] = dot(pick, rret[b, :rows], 0, 0).astype(BF16)

    def weight_grad(k):
        wide = ff // 4
        cols = slice(k * wide, (k + 1) * wide)
        sums = []
        for h in range(2):
            left = jnp.concatenate([blocks(xin, b, h, slice(0, feat)) for b in range(BATCHES)], 0)
            right = jnp.concatenate([blocks(hg, b, h, cols) for b in range(BATCHES)], 0)
            sums.append(dot(left, right, 0, 0))
        flip = swap(sums[0].shape)
        gup[0, :, cols] = jnp.where(flip, sums[1], sums[0]).astype(BF16)
        gup[1, :, cols] = jnp.where(flip, sums[0], sums[1]).astype(BF16)

    def rs_copy(way, d, q):
        src = pos(sign[1 - way] * d) * count + q * quarter
        return send(
            ptok.at[pl.ds(src, quarter)], rs.at[way, d - 1, pl.ds(q * quarter, quarter)],
            rsem.at[way, d - 1, q], z_to[way],
        )

    def rs_has(way, d, q):
        return d < half or (d == half and q // 2 == 1 - way)

    pieces = [(way, q) for p in range(2) for way, q in ((1, p), (0, 2 + p))]
    pieces = pieces + [(1 - way, q) for way, q in pieces]

    def rs_start():
        for way, q in pieces:
            if rs_has(way, half, q):
                rs_copy(way, half, q).start()
        for way, q in pieces:
            if not rs_has(way, half, q):
                rs_copy(way, half - 1, q).start()

    def rs_step(d):
        for way, q in pieces[4:] + pieces[:4]:
            if not rs_has(way, d + 1, q):
                continue
            rs_copy(way, d + 1, q).wait_recv()
            at = pos(sign[1 - way] * d) * count + q * quarter
            arrived = rs[way, d, q * quarter : (q + 1) * quarter].astype(F32)
            ptok[at : at + quarter] = (ptok[at : at + quarter].astype(F32) + arrived).astype(BF16)
            rs_copy(way, d, q).start()

    def rs_end():
        for q in range(4):
            total = ptok[mine + q * quarter : mine + (q + 1) * quarter].astype(F32)
            for way in (1, 0):
                rs_copy(way, 1, q).wait_recv()
                total = total + rs[way, 0, q * quarter : (q + 1) * quarter].astype(F32)
            gtok_ref[q * quarter : (q + 1) * quarter] = total.astype(BF16)

    def ms_copy(way, d):
        src = pos(sign[1 - way] * d)
        return send(
            pmix.at[pl.ds(src * count, count)], ms.at[way, d - 1], msem.at[way, d - 1], z_to[way]
        )

    def gs_copy(way, d):
        src = pos(sign[1 - way] * d)
        return send(pgg.at[src], gs.at[way, d - 1], gsem.at[way, d - 1], z_to[way])

    def ms_has(way, d):
        return d < half or (d == half and way == 1)

    def ms_step(d):
        for way in (1, 0):
            if not ms_has(way, d):
                continue
            if ms_has(way, d + 1):
                src = pos(sign[1 - way] * d)
                ms_copy(way, d + 1).wait_recv()
                at = slice(src * count, (src + 1) * count)
                pmix[at] = (pmix[at].astype(F32) + ms[way, d].astype(F32)).astype(BF16)
                gs_copy(way, d + 1).wait_recv()
                pgg[src] = pgg[src] + gs[way, d]
            ms_copy(way, d).start()
            gs_copy(way, d).start()

    def tx_core():
        return send(gx.at[0], gx.at[1], txsem.at[0], other)

    def tx_copy(i):
        return send(gx.at[2], gx.at[2 + i], txsem.at[i], x_to[i])

    def ms_end():
        total = pmix[mine : mine + count].astype(F32)
        gates = pgg[pos(0)]
        for way in (1, 0):
            ms_copy(way, 1).wait_recv()
            total = total + ms[way, 0].astype(F32)
            gs_copy(way, 1).wait_recv()
            gates = gates + gs[way, 0]
        mixed_ref[...] = total.astype(BF16)
        gx[0] = gates
        tx_core().start()

    def tx_middle():
        tx_core().wait_recv()
        gx[2] = gx[0] + gx[1]
        for i in range(1, nx):
            tx_copy(i).start()

    def tx_end():
        total = gx[2]
        for i in range(1, nx):
            tx_copy(i).wait_recv()
            total = total + gx[2 + i]
        ggate_ref[...] = total

    def order_weights():
        load.wait()
        for k in range(4):
            cols = slice(k * (ff // 4), (k + 1) * (ff // 4))
            first, second = wraw[0, :, cols].astype(F32), wraw[1, :, cols].astype(F32)
            flip = swap(first.shape)
            wsel[0, :, cols] = jnp.where(flip, second, first).astype(BF16)
            wsel[1, :, cols] = jnp.where(flip, first, second).astype(BF16)

    stage = {
        "g": gather, "f": forward, "p": pair_sum, "m": middle, "h": hg_forward, "x": mix,
        "b": backward, "s": scatter, "w": weight_grad, "M": ms_step, "R": rs_step,
    }

    def run(jobs):
        for job in jobs.split():
            stage[job[0]](int(job[1:]))

    ag_start()
    order_weights()
    for s in range(1, half + 1):
        for q in range(4):
            ag_step(s, q)
            run(DURING.get((s, q), ""))
    run(BETWEEN)
    rs_start()
    run("s2 R7 M4 R6 M3 R5 M2 w0 R4 M1 w1 R3")
    ms_end()
    run("w2 R2")
    tx_middle()
    run("w3")
    tx_end()
    store = pltpu.make_async_copy(gup, gup_hbm, osem)
    store.start()
    run("R1")
    rs_end()
    store.wait()

    for s in range(1, half + 1):
        for way in (0, 1):
            for q in range(4):
                if ag_has(way, s, q):
                    ag_copy(way, s, q).wait_send()
            if ag_info_has(way, s):
                ag_info(way, s).wait_send()
    for d in range(1, half + 1):
        for way, q in pieces:
            if rs_has(way, d, q):
                rs_copy(way, d, q).wait_send()
        for way in (0, 1):
            if ms_has(way, d):
                ms_copy(way, d).wait_send()
                gs_copy(way, d).wait_send()
    for b in range(BATCHES):
        for copy in y_copies(b, ysem, xsend, xin, y_to):
            copy.wait_send()
        for copy in y_copies(b, asem, act, aret, y_back):
            copy.wait_send()
        for copy in y_copies(b, bsem, brow, rret, y_back):
            copy.wait_send()
        core_copy(b).wait_send()
        for i in range(nx):
            hg_core(b, i).wait_send()
            if i > 0:
                x_copy(b, i).wait_send()
                hg_x(b, i).wait_send()
    tx_core().wait_send()
    for i in range(1, nx):
        tx_copy(i).wait_send()


def copy_kernel(*refs):
    count = (len(refs) - 1) // 3
    sources, targets, held, sems = refs[:count], refs[count : 2 * count], refs[2 * count : -1], refs[-1]
    pieces = []
    for k in range(count):
        depth = sources[k].shape[0]
        cuts = PIECES if depth % (16 * PIECES) == 0 and depth > 128 else 1
        for i in range(cuts):
            rows = pl.ds(i * (depth // cuts), depth // cuts)
            pieces.append((sources[k].at[rows], held[k].at[rows], targets[k].at[rows]))
    loads = [pltpu.make_async_copy(a, b, sems.at[0, i]) for i, (a, b, c) in enumerate(pieces)]
    stores = [pltpu.make_async_copy(b, c, sems.at[1, i]) for i, (a, b, c) in enumerate(pieces)]
    for load in loads:
        load.start()
    for load, store in zip(loads, stores):
        load.wait()
        store.start()
    for store in stores:
        store.wait()


def on_device(ny, tokens, routes, gates, up_weight, replica_on, grad_out):
    count, feat = tokens.shape
    topk = routes.shape[1]
    share = grad_out.shape[1]
    ff = up_weight.shape[2]
    experts = replica_on.shape[0]
    nz = lax.axis_size("ep") // ny
    nx = lax.axis_size("tp") // 2
    half = nz // 2
    rows = ny * sum(block_rows(max(SIZES)))
    slots = max(SIZES) * count
    vmem = pl.BlockSpec(memory_space=pltpu.VMEM)
    hbm = pl.BlockSpec(memory_space=pl.ANY)

    def dma(*shape):
        return pltpu.SemaphoreType.DMA(shape + (2,))

    out_shape = [
        jax.ShapeDtypeStruct((count, share), BF16),
        jax.ShapeDtypeStruct((count, feat), BF16),
        jax.ShapeDtypeStruct((topk, count), F32),
        jax.ShapeDtypeStruct(up_weight.shape, BF16),
    ]
    outs = pl.pallas_call(
        functools.partial(kernel, (ny, nz, nx)),
        out_shape=out_shape,
        in_specs=[vmem] * 5 + [hbm],
        out_specs=[vmem] * 3 + [hbm],
        scratch_shapes=[
            pltpu.VMEM((2 * ny, count), F32),
            pltpu.VMEM((2 * ny, count), F32),
            pltpu.VMEM((nz * count, feat + share), BF16),
            pltpu.VMEM((nz, 2 * topk, count), F32),
            pltpu.VMEM(up_weight.shape, BF16),
            pltpu.VMEM(up_weight.shape, BF16),
            pltpu.VMEM((BATCHES, rows, slots), BF16),
            pltpu.VMEM((BATCHES, rows, share), F32),
            pltpu.VMEM((BATCHES, rows, share), BF16),
            pltpu.VMEM((BATCHES, rows, feat + share), BF16),
            pltpu.VMEM((BATCHES, rows, feat + share), BF16),
            pltpu.VMEM((BATCHES, 2, nx, rows, share), BF16),
            pltpu.VMEM((BATCHES, nx, rows, share), BF16),
            pltpu.VMEM((BATCHES, nx, rows, share), BF16),
            pltpu.VMEM((BATCHES, nx, rows, share), BF16),
            pltpu.VMEM((BATCHES, rows, share), BF16),
            pltpu.VMEM((BATCHES, rows, share), BF16),
            pltpu.VMEM((BATCHES, rows, share), BF16),
            pltpu.VMEM((BATCHES, rows, ff), BF16),
            pltpu.VMEM((BATCHES, rows, feat), BF16),
            pltpu.VMEM((BATCHES, rows, feat), BF16),
            pltpu.VMEM((nz * count, feat), BF16),
            pltpu.VMEM((2, half, count, feat), BF16),
            pltpu.VMEM((nz * count, share), BF16),
            pltpu.VMEM((2, half, count, share), BF16),
            pltpu.VMEM((nz, topk, count), F32),
            pltpu.VMEM((2, half, topk, count), F32),
            pltpu.VMEM(up_weight.shape, BF16),
            pltpu.VMEM((2 + nx, topk, count), F32),
            pltpu.SemaphoreType.DMA,
            pltpu.SemaphoreType.DMA,
            pltpu.SemaphoreType.DMA((BATCHES,)),
            dma(2, half, 4),
            dma(2, half),
            dma(BATCHES, ny),
            dma(BATCHES),
            dma(BATCHES, nx),
            dma(BATCHES, ny),
            dma(BATCHES, nx),
            dma(BATCHES, nx),
            dma(BATCHES, ny),
            dma(2, half, 4),
            dma(2, half),
            dma(2, half),
            dma(nx),
        ],
        compiler_params=pltpu.CompilerParams(
            collective_id=0, has_side_effects=True, vmem_limit_bytes=56 * 1024 * 1024
        ),
        cost_estimate=pl.CostEstimate(
            flops=32 * rows * feat * ff, bytes_accessed=8 * feat * ff, transcendentals=8 * rows * share
        ),
    )(routes.T, gates.T, replica_on[None, :], tokens, grad_out, up_weight)
    flat = jax.ShapeDtypeStruct((up_weight.shape[0] * feat, ff), BF16)
    out_shape = [*out_shape[:3], flat]
    mixed, gtok, ggate, gup = pl.pallas_call(
        copy_kernel,
        out_shape=out_shape,
        in_specs=[hbm] * 4,
        out_specs=[hbm] * 4,
        scratch_shapes=[pltpu.VMEM(o.shape, o.dtype) for o in out_shape]
        + [pltpu.SemaphoreType.DMA((2, 3 + PIECES))],
        compiler_params=pltpu.CompilerParams(vmem_limit_bytes=16 * 1024 * 1024),
    )(*outs[:3], outs[3].reshape(flat.shape))
    gup = gup.reshape(up_weight.shape)
    return mixed, gtok, ggate.T, gup


def solution(mesh, ny=NY):
    return jax.shard_map(
        functools.partial(on_device, ny),
        mesh=mesh,
        in_specs=(
            P("ep", "tp"), P("ep", None), P("ep", None), P("ep", "tp", None), P(), P("ep", "tp"),
        ),
        out_specs=(P("ep", "tp"), P("ep", "tp"), P("ep", None), P("ep", "tp", None)),
        check_vma=False,
    )
```

time: 154 us -> 128 us (0.83)
  Pallas kernels: 141 us -> 122 us
  local copies, waits for them, and re-layouts: 8.55 us -> 3.93 us
  other arithmetic: 2.85 us -> 0 us
    pallas_call x1 -> x2, Pallas kernels: 141 us -> 122 us  [the longest x1 120 us: on_device(): pl.pallas_call(functools.partial(kernel, (ny, nz, nx)), out_shape=out_sha...]
    unnamed x4 -> x8, local copies, waits for them, and re-layouts: 7.29 us -> 3.93 us
where the time goes in v3:
time: 128 us; the launch traced here: 126 us
  Pallas kernels  122 us (95%)
  local copies, waits for them, and re-layouts  3.93 us (3%)
    pallas_call x1, Pallas kernels, on_device(): pl.pallas_call(functools.partial(kernel, (ny, nz, nx)), out_shape=out_sha...  120 us
    unnamed x8, local copies, waits for them, and re-layouts  3.93 us

profile of v3, /device:TPU:1, one launch (start us, length us, event | category | flops | bytes accessed | tf_op | source)
XLA Modules:
  0.0 126.5 jit_solution(6503680074336557949)
XLA Ops:
  0.6 119.8 %shard_map.93 = (bf16[128,128]{1,0:T(8,128)(2,1)}, bf16[128,512]{1,0:T(8,128)(2,1)}, f32[8,128]{1,0:T(8,128)}, bf16[2,512,1024]{2,1,0:T(8,128)(2,1)}) custom-call(s32[8,128]{1,0:T(8,128)} %bitcast.8, f32[8,128]{1,0:T(8,128)} %bitcast.9, s32[1,128]{1,0:T(1,128)} %bitcast.11, bf16[128,512]{1,0:T(8,128)(2,1)} %tokens_ref.1, bf16[128,128]{1,0:T(8,128)(2,1)} %grad_ref.1, ...), custom_call_target="tpu_custom_call" | custom-call | flops 5368709120 | bytes 4194304 | tf_op jit(solution)/shard_map/pallas_call | solution.py:568
  120.5 0.0 copy-start
  120.5 1.6 %copy-done = bf16[2,512,1024]{2,1,0:T(8,128)(2,1)S(1)} copy-done((bf16[2,512,1024]{2,1,0:T(8,128)(2,1)S(1)}, bf16[2,512,1024]{2,1,0:T(8,128)(2,1)}, u32[]{:S(2)}) %copy-start) | copy-done | bytes 2097176
  122.1 0.0 copy-start.1
  122.1 0.9 copy-done.1
  123.0 0.0 copy-start.2
  123.0 0.8 copy-done.2
  123.7 0.0 copy-start.3
  123.7 0.7 copy-done.3
  124.4 1.9 %shard_map.94 = (bf16[128,128]{1,0:T(8,128)(2,1)}, bf16[128,512]{1,0:T(8,128)(2,1)}, f32[8,128]{1,0:T(8,128)}, bf16[1024,1024]{1,0:T(8,128)(2,1)}) custom-call(bf16[128,128]{1,0:T(8,128)(2,1)S(1)} %copy-done.2, bf16[128,512]{1,0:T(8,128)(2,1)S(1)} %copy-done.1, f32[8,128]{1,0:T(8,128)S(1)} %copy-done.3, bf16[1024,1024]{1,0:T(8,128)(2,1)S(1)} %bitcast.6), custom_call_target="tpu_custom_call" | custom-call | tf_op jit(solution)/shard_map/pallas_call | solution.py:629
Async XLA Ops:
  120.5 1.6 %copy-start = (bf16[2,512,1024]{2,1,0:T(8,128)(2,1)S(1)}, bf16[2,512,1024]{2,1,0:T(8,128)(2,1)}, u32[]{:S(2)}) copy-start(bf16[2,512,1024]{2,1,0:T(8,128)(2,1)} %get-tuple-element.15) | copy-start | bytes 6291460
  122.1 0.9 copy-start.1
  123.0 0.8 copy-start.2
  123.7 0.7 copy-start.3

commit v4 on v3

--- a/solution.py
+++ b/solution.py
@@ -38,12 +38,11 @@
 
 
 DURING = {
-    (2, 3): "g0", (4, 2): "f0", (4, 3): "g1", (5, 0): "p0", (6, 1): "m0", (6, 2): "f1",
-    (6, 3): "g2", (7, 0): "p1", (7, 2): "h0", (7, 3): "g3", (8, 0): "b0", (8, 1): "m1 f2",
-    (8, 3): "g4",
+    (2, 3): "g0", (4, 3): "g1 f0", (5, 1): "p0", (6, 3): "g2 m0", (7, 0): "f1", (7, 2): "p1",
+    (7, 3): "g3", (8, 3): "g4",
 }
 BETWEEN = (
-    "p2 f3 x0 p3 s0 f4 h1 x1 p4 m2 m3 b1 m4 h2 x2 x3 h3 b2 b3 s1 x4 M8 h4 M7 b4 M6 s3 M5 s4"
+    "f3 f2 p3 p2 h0 x0 b0 A0 f4 p4 m3 s0 m4 m2 h3 x3 b3 m1 x4 M8 h4 M7 b4 h2 x2 s3 b2 M6 s4"
 )
 
 
@@ -177,7 +176,7 @@
                 src.at[b, pl.ds(j * block, block)], dst.at[b, pl.ds(j * block, block)],
                 sems.at[b, j], to[j],
             )
-            for j in range(1, ny)
+            for j in sorted(range(1, ny), key=lambda j: -min(j, ny - j))
         ]
 
     def gather(b):
@@ -251,7 +250,7 @@
 
     def pair_sum(b):
         core_copy(b).wait_recv()
-        for i in [*range(1, nx), 0]:
+        for i in [*sorted(range(1, nx), key=lambda i: -min(i, nx - i)), 0]:
             to = lax.rem(x + i, nx)
             rows = slice(0, rows_of[b])
             total = part[b, c, to, rows].astype(F32) + pin[b, to, rows].astype(F32)
@@ -459,51 +458,16 @@
             wsel[0, :, cols] = jnp.where(flip, second, first).astype(BF16)
             wsel[1, :, cols] = jnp.where(flip, first, second).astype(BF16)
 
-    stage = {
-        "g": gather, "f": forward, "p": pair_sum, "m": middle, "h": hg_forward, "x": mix,
-        "b": backward, "s": scatter, "w": weight_grad, "M": ms_step, "R": rs_step,
-    }
-
-    def run(jobs):
-        for job in jobs.split():
-            stage[job[0]](int(job[1:]))
-
-    ag_start()
-    order_weights()
-    for s in range(1, half + 1):
-        for q in range(4):
-            ag_step(s, q)
-            run(DURING.get((s, q), ""))
-    run(BETWEEN)
-    rs_start()
-    run("s2 R7 M4 R6 M3 R5 M2 w0 R4 M1 w1 R3")
-    ms_end()
-    run("w2 R2")
-    tx_middle()
-    run("w3")
-    tx_end()
-    store = pltpu.make_async_copy(gup, gup_hbm, osem)
-    store.start()
-    run("R1")
-    rs_end()
-    store.wait()
-
-    for s in range(1, half + 1):
-        for way in (0, 1):
-            for q in range(4):
-                if ag_has(way, s, q):
-                    ag_copy(way, s, q).wait_send()
-            if ag_info_has(way, s):
-                ag_info(way, s).wait_send()
-    for d in range(1, half + 1):
-        for way, q in pieces:
-            if rs_has(way, d, q):
-                rs_copy(way, d, q).wait_send()
-        for way in (0, 1):
-            if ms_has(way, d):
-                ms_copy(way, d).wait_send()
-                gs_copy(way, d).wait_send()
-    for b in range(BATCHES):
+    def drain_gather(_):
+        for s in range(1, half + 1):
+            for way in (0, 1):
+                for q in range(4):
+                    if ag_has(way, s, q):
+                        ag_copy(way, s, q).wait_send()
+                if ag_info_has(way, s):
+                    ag_info(way, s).wait_send()
+
+    def drain_batch(b):
         for copy in y_copies(b, ysem, xsend, xin, y_to):
             copy.wait_send()
         for copy in y_copies(b, asem, act, aret, y_back):
@@ -516,6 +480,49 @@
             if i > 0:
                 x_copy(b, i).wait_send()
                 hg_x(b, i).wait_send()
+
+    def drain_sums(far):
+        for d in far:
+            for way, q in pieces:
+                if rs_has(way, d, q):
+                    rs_copy(way, d, q).wait_send()
+            for way in (0, 1):
+                if ms_has(way, d):
+                    ms_copy(way, d).wait_send()
+                    gs_copy(way, d).wait_send()
+
+    stage = {
+        "g": gather, "f": forward, "p": pair_sum, "m": middle, "h": hg_forward, "x": mix,
+        "b": backward, "s": scatter, "w": weight_grad, "M": ms_step, "R": rs_step,
+        "A": drain_gather, "D": drain_batch,
+    }
+
+    def run(jobs):
+        for job in jobs.split():
+            stage[job[0]](int(job[1:]))
+
+    ag_start()
+    order_weights()
+    for s in range(1, half + 1):
+        for q in range(4):
+            ag_step(s, q)
+            run(DURING.get((s, q), ""))
+    run(BETWEEN)
+    rs_start()
+    run("h1 x1 b1 R7 s2 M5 R6 M4 R5 s1 M3 R4 M2 R3 M1")
+    ms_end()
+    run("w0 w1 R2")
+    tx_middle()
+    run("D0 w2 D1 D2 w3 D3 D4")
+    tx_end()
+    store = pltpu.make_async_copy(gup, gup_hbm, osem)
+    store.start()
+    run("R1")
+    drain_sums(range(2, half + 1))
+    rs_end()
+    store.wait()
+
+    drain_sums((1,))
     tx_core().wait_send()
     for i in range(1, nx):
         tx_copy(i).wait_send()
@@ -633,7 +640,7 @@
         out_specs=[hbm] * 4,
         scratch_shapes=[pltpu.VMEM(o.shape, o.dtype) for o in out_shape]
         + [pltpu.SemaphoreType.DMA((2, 3 + PIECES))],
-        compiler_params=pltpu.CompilerParams(vmem_limit_bytes=16 * 1024 * 1024),
+        compiler_params=pltpu.CompilerParams(vmem_limit_bytes=56 * 1024 * 1024),
     )(*outs[:3], outs[3].reshape(flat.shape))
     gup = gup.reshape(up_weight.shape)
     return mixed, gtok, ggate.T, gup

time: 128 us -> 119 us (0.930)
  Pallas kernels: 122 us -> 118 us
  local copies, waits for them, and re-layouts: 3.93 us -> 0 us
    pallas_call x1, Pallas kernels: 120 us -> 115 us  [on_device(): pl.pallas_call(functools.partial(kernel, (ny, nz, nx)), out_shape=out_sha...]
    unnamed x8 -> x0, local copies, waits for them, and re-layouts: 3.93 us -> none
where the time goes in v4:
time: 119 us; the launch traced here: 118 us
  Pallas kernels  118 us (99%)
    pallas_call x1, Pallas kernels, on_device(): pl.pallas_call(functools.partial(kernel, (ny, nz, nx)), out_shape=out_sha...  115 us
    pallas_call x1, Pallas kernels, on_device(): pl.pallas_call(copy_kernel, out_shape=out_shape, in_specs=[hbm] * 4, out_...  2.54 us

profile of v4, /device:TPU:1, one launch (start us, length us, event | category | flops | bytes accessed | tf_op | source)
XLA Modules:
  0.0 118.3 jit_solution(6363958902167941414)
XLA Ops:
  0.6 115.0 %shard_map.93 = (bf16[128,128]{1,0:T(8,128)(2,1)}, bf16[128,512]{1,0:T(8,128)(2,1)}, f32[8,128]{1,0:T(8,128)}, bf16[2,512,1024]{2,1,0:T(8,128)(2,1)}) custom-call(s32[8,128]{1,0:T(8,128)} %bitcast.8, f32[8,128]{1,0:T(8,128)} %bitcast.9, s32[1,128]{1,0:T(1,128)} %bitcast.11, bf16[128,512]{1,0:T(8,128)(2,1)} %tokens_ref.1, bf16[128,128]{1,0:T(8,128)(2,1)} %grad_ref.1, ...), custom_call_target="tpu_custom_call" | custom-call | flops 5368709120 | bytes 4194304 | tf_op jit(solution)/shard_map/pallas_call | solution.py:575
  115.6 2.5 %shard_map.94 = (bf16[128,128]{1,0:T(8,128)(2,1)}, bf16[128,512]{1,0:T(8,128)(2,1)}, f32[8,128]{1,0:T(8,128)}, bf16[1024,1024]{1,0:T(8,128)(2,1)}) custom-call(bf16[128,128]{1,0:T(8,128)(2,1)} %get-tuple-element.12.refs_0_, bf16[128,512]{1,0:T(8,128)(2,1)} %get-tuple-element.13.refs_1_, f32[8,128]{1,0:T(8,128)} %get-tuple-element.14.refs_2_, ...), custom_call_target="tpu_custom_call" | custom-call | tf_op jit(solution)/shard_map/pallas_call | solution.py:636
